TPU v7x, 128 devices: a whole 4x4x4 slice. The times are simulated.
128 devices in a mesh: pair: 32 (over z_lo, x, y), row: 4 (over z_hi, core).
Axes of the slice: x: 4, y: 4, z: 4 (z_hi: 2, z_lo: 2; z = z_hi * 2 + z_lo), core: 2. Of those that a mesh axis runs over, the one named last changes fastest.
Arguments:
- factor: float32 [16384, 16384], P('row', 'pair'), may hold values from -90 to 90
Outputs:
- rotated: float32 [16384, 16384], P('row', 'pair')
All inputs are finite; a program needn't handle non-finite values.
Results may differ from a plain program's by a relative error of at most 0.0003.
Values sent between devices are 32-bit elements; how exact they have to be, the bound alone decides.
No kernel may reach another device: no remote copies, remote signals or barrier semaphores. Data moves between devices by JAX's collectives and lax.ppermute only.
A program may use at most 128 MiB of HBM per device.

v0:
```python
import jax
import jax.numpy as jnp
from jax import lax
from jax.sharding import PartitionSpec as P

B = 128
STEPS = 4
ITERS = 12


EPS = 1e-06
DAMPING = 0.04
HIGH = lax.Precision.HIGHEST


def shifted(value, axis, steps):
    count = lax.axis_size(axis)
    initial, last = (max(0, -steps), min(count, count - steps))
    return lax.ppermute(value, axis, [(source, source + steps) for source in range(initial, last)])


def coupling_from(gram, norm_top, norm_bottom):
    differ = norm_top[:, :, None] - norm_bottom[:, None, :]
    total = norm_top[:, :, None] + norm_bottom[:, None, :] + EPS
    radius = jnp.sqrt(differ * differ + 4.0 * gram * gram)
    denominator = differ * differ + jnp.abs(differ) * radius + DAMPING * total * total
    return -2.0 * gram * differ / denominator


def polar_from(coupling):
    eye = jnp.eye(coupling.shape[0], dtype=jnp.float32)
    upper = jnp.concatenate([eye, coupling], axis=1)
    lower = jnp.concatenate([-coupling.T, eye], axis=1)
    scale = lax.rsqrt(1.0 + jnp.sum(coupling * coupling))
    matrix = jnp.concatenate([upper, lower], axis=0) * scale
    for index in range(ITERS):
        inner = jnp.dot(matrix.T, matrix, precision=HIGH)
        matrix = 1.5 * matrix - 0.5 * jnp.dot(matrix, inner, precision=HIGH)
    return matrix


def pass_edges(top_last, bottom_first):
    incoming_top = shifted(top_last, "pair", 1)
    incoming_bottom = shifted(bottom_first, "pair", -1)
    return (incoming_top, incoming_bottom)


def arrange(top, bottom, incoming_top, incoming_bottom, is_first, is_last):
    leading = jnp.where(is_first, top[:, 0], incoming_top)
    second = jnp.where(is_first, bottom[:, 0], top[:, 0])
    new_top = jnp.concatenate([leading[:, None], second[:, None], top[:, 1:-1]], axis=1)
    trailing = jnp.where(is_last, top[:, -1], incoming_bottom)
    new_bottom = jnp.concatenate([bottom[:, 1:], trailing[:, None]], axis=1)
    return jnp.concatenate([new_top, new_bottom], axis=2)


def per_device(factor):
    rows, columns = factor.shape
    pair_dev = columns // (2 * B)
    joined = factor.reshape(rows, pair_dev, 2 * B)
    position = lax.axis_index("pair")
    is_first = position == 0
    is_last = position == lax.axis_size("pair") - 1
    for step in range(STEPS):
        top = joined[:, :, :B]
        bottom = joined[:, :, B:]
        gram = jnp.einsum("mpi,mpj->pij", top, bottom, precision=HIGH)
        norm_top = jnp.sum(top * top, axis=0)
        norm_bottom = jnp.sum(bottom * bottom, axis=0)
        gram, norm_top, norm_bottom = lax.psum((gram, norm_top, norm_bottom), "row")
        coupling = coupling_from(gram, norm_top, norm_bottom)
        polar = jax.vmap(polar_from)(coupling)
        if step == STEPS - 1:
            joined = jnp.einsum("mpa,pab->mpb", joined, polar, precision=HIGH)
        else:
            joined = jnp.einsum("mpa,pab->mpb", joined, polar, precision=HIGH)
            top = joined[:, :, :B]
            bottom = joined[:, :, B:]
            incoming_top, incoming_bottom = pass_edges(top[:, -1], bottom[:, 0])
            joined = arrange(top, bottom, incoming_top, incoming_bottom, is_first, is_last)
    return joined.reshape(rows, columns)


def solution(mesh):
    placed = (P("row", "pair"),)
    return jax.shard_map(
        per_device, mesh=mesh, in_specs=placed, out_specs=P("row", "pair"), check_vma=False
    )
```

profile of v0, /device:TPU:30, one launch (start us, length us, event | category | flops | bytes accessed | tf_op | source)
XLA Modules:
  0.0 533.3 jit_solution(15841290192127488245)
XLA Ops:
  6.5 8.9 %copy.123 = f32[4096,512]{0,1:T(8,128)} copy(f32[4096,512]{1,0:T(8,128)} %param.1) | data formatting | bytes 16777216 | tf_op args[0]
  15.4 8.1 %fusion.30 = f32[2,128,128]{2,1,0:T(8,128)} fusion(f32[4096,2,256]{0,2,1:T(8,128)} %bitcast.245), kind=kOutput, calls=%fused_computation.41 | convolution fusion | flops 1610612736 | bytes 8519680 | tf_op jit(solution)/shard_map/mpi,mpj->pij/dot_general | solution.py:67
  23.6 6.2 %multiply_reduce_fusion.7 = (f32[2,128]{1,0:T(2,128)S(1)}, f32[4096,2,128]{0,2,1:T(8,128)}) fusion(f32[4096,2,256]{0,2,1:T(8,128)} %bitcast.246), kind=kLoop, calls=%fused_computation.40 | loop fusion | flops 2096896 | bytes 12583936 | tf_op jit(solution)/shard_map/reduce_sum | solution.py:68
  29.8 5.6 %copy.302 = f32[4096,2,128]{2,0,1:T(8,128)} copy(f32[4096,2,128]{0,2,1:T(8,128)} %get-tuple-element.40) | data formatting | bytes 8388608
  38.1 11.0 %all-reduce.3 = (f32[2,128]{1,0:T(2,128)S(1)}, f32[2,128]{1,0:T(2,128)S(1)}) all-reduce(f32[2,128]{1,0:T(2,128)S(1)} %multiply_reduce_fusion.6, f32[2,128]{1,0:T(2,128)S(1)} %get-tuple-element.39), channel_id=1, replica_groups=mesh['pair'=32,'row'=4] {'row'}, use_global_device_ids=true, to_apply=%region_4.0 | all-reduce | flops 512 | bytes 4096 | tf_op jit(solution)/shard_map/psum | solution.py:70
  49.1 16.8 %all-reduce.9.cloned.1.call-done = f32[2,128,128]{2,1,0:T(8,128)} async-done(((f32[2,128,128]{2,1,0:T(8,128)}), f32[2,128,128]{2,1,0:T(8,128)}) %all-reduce.9.cloned.1.call-update) | async-done | bytes 131088 | tf_op jit(solution)/shard_map/psum | solution.py:70
  89.4 8.8 %convolution_bitcast_fusion = f32[4096,2,256]{0,2,1:T(8,128)S(1)} fusion(f32[2,256,256]{1,2,0:T(8,128)S(1)} %fusion.74, f32[4096,2,256]{0,2,1:T(8,128)S(1)} %bitcast.249), kind=kOutput, calls=%fused_computation.26 | convolution fusion | flops 6442450944 | bytes 17301504 | tf_op jit(solution)/shard_map/mpa,pab->mpb/dot_general | solution.py:76
  109.4 44.1 %collective-permute-done = f32[4096,128]{0,1:T(8,128)} collective-permute-done((f32[4096,128]{0,1:T(8,128)}, f32[4096,128]{0,1:T(8,128)}, u32[]{:S(2)}, u32[]{:S(2)}) %collective-permute-start) | collective-permute-done | bytes 2097184 | tf_op jit(solution)/shard_map/ppermute | solution.py:19
  153.5 6.4 %collective-permute-done.1 = f32[4096,128]{0,1:T(8,128)} collective-permute-done((f32[4096,128]{0,1:T(8,128)}, f32[4096,128]{0,1:T(8,128)}, u32[]{:S(2)}, u32[]{:S(2)}) %collective-permute-start.1) | collective-permute-done | bytes 2097184 | tf_op jit(solution)/shard_map/ppermute | solution.py:19
  174.1 8.0 %all-reduce.2 = (f32[2,128]{1,0:T(2,128)S(1)}, f32[2,128]{1,0:T(2,128)S(1)}) all-reduce(f32[2,128]{1,0:T(2,128)S(1)} %get-tuple-element.46, f32[2,128]{1,0:T(2,128)S(1)} %get-tuple-element.47), channel_id=1, replica_groups=mesh['pair'=32,'row'=4] {'row'}, use_global_device_ids=true, to_apply=%region_10.11 | all-reduce | flops 512 | bytes 4096 | tf_op jit(solution)/shard_map/psum | solution.py:70
  182.1 28.5 %all-reduce.11.cloned.1.call-done = f32[2,128,128]{1,2,0:T(8,128)} async-done(((f32[2,128,128]{1,2,0:T(8,128)}), f32[2,128,128]{1,2,0:T(8,128)}) %all-reduce.11.cloned.1.call-update) | async-done | bytes 131088 | tf_op jit(solution)/shard_map/psum | solution.py:70
  233.7 8.8 %fusion.27 = f32[4096,2,256]{0,2,1:T(8,128)S(1)} fusion(f32[2,256,256]{2,1,0:T(8,128)S(1)} %fusion.62, f32[4096,1,128]{0,2,1:T(8,128)S(1)} %copy-done.10, f32[4096,1,128]{0,2,1:T(8,128)S(1)} %get-tuple-element.37, f32[4096,1,128]{0,2,1:T(8,128)S(1)} %copy-done.2, f32[4096,1,128]{0,2,1:T(8,128)S(1)} %copy-done.8), kind=kOutput, calls=%fused_computation.25 | convolution fusion | flops 6448742400 | bytes 17301504 | tf_op jit(solution)/shard_map/mpa,pab->mpb/dot_general | solution.py:76
  249.4 43.9 %collective-permute-done.2 = f32[4096,128]{0,1:T(8,128)S(1)} collective-permute-done((f32[4096,128]{0,1:T(8,128)S(1)}, f32[4096,128]{0,1:T(8,128)S(1)}, u32[]{:S(2)}, u32[]{:S(2)}) %collective-permute-start.2) | collective-permute-done | bytes 2097184 | tf_op jit(solution)/shard_map/ppermute | solution.py:19
  293.3 6.4 %collective-permute-done.3 = f32[4096,128]{0,1:T(8,128)S(1)} collective-permute-done((f32[4096,128]{0,1:T(8,128)S(1)}, f32[4096,128]{0,1:T(8,128)S(1)}, u32[]{:S(2)}, u32[]{:S(2)}) %collective-permute-start.3) | collective-permute-done | bytes 2097184 | tf_op jit(solution)/shard_map/ppermute | solution.py:19
  310.6 8.0 %all-reduce.1 = (f32[2,128]{1,0:T(2,128)S(1)}, f32[2,128]{1,0:T(2,128)S(1)}) all-reduce(f32[2,128]{1,0:T(2,128)S(1)} %multiply_reduce_fusion.2, f32[2,128]{1,0:T(2,128)S(1)} %multiply_reduce_fusion.3), channel_id=1, replica_groups=mesh['pair'=32,'row'=4] {'row'}, use_global_device_ids=true, to_apply=%region_16.17 | all-reduce | flops 512 | bytes 4096 | tf_op jit(solution)/shard_map/psum | solution.py:70
  318.7 28.4 %all-reduce.13.cloned.1.call-done = f32[2,128,128]{1,2,0:T(8,128)} async-done(((f32[2,128,128]{1,2,0:T(8,128)}), f32[2,128,128]{1,2,0:T(8,128)}) %all-reduce.13.cloned.1.call-update) | async-done | bytes 131088 | tf_op jit(solution)/shard_map/psum | solution.py:70
  370.1 8.8 %fusion.24 = f32[4096,2,256]{0,2,1:T(8,128)S(1)} fusion(f32[2,256,256]{2,1,0:T(8,128)S(1)} %fusion.50, f32[4096,1,128]{0,2,1:T(8,128)S(1)} %copy-done.15, f32[4096,1,128]{0,2,1:T(8,128)S(1)} %get-tuple-element.31, f32[4096,1,128]{0,2,1:T(8,128)S(1)} %copy-done.4, f32[4096,1,128]{0,2,1:T(8,128)S(1)} %copy-done.12), kind=kOutput, calls=%fused_computation.24 | convolution fusion | flops 6448742400 | bytes 17301504 | tf_op jit(solution)/shard_map/mpa,pab->mpb/dot_general | solution.py:76
  385.8 43.9 %collective-permute-done.4 = f32[4096,128]{0,1:T(8,128)S(1)} collective-permute-done((f32[4096,128]{0,1:T(8,128)S(1)}, f32[4096,128]{0,1:T(8,128)S(1)}, u32[]{:S(2)}, u32[]{:S(2)}) %collective-permute-start.4) | collective-permute-done | bytes 2097184 | tf_op jit(solution)/shard_map/ppermute | solution.py:19
  429.7 6.4 %collective-permute-done.5 = f32[4096,128]{0,1:T(8,128)S(1)} collective-permute-done((f32[4096,128]{0,1:T(8,128)S(1)}, f32[4096,128]{0,1:T(8,128)S(1)}, u32[]{:S(2)}, u32[]{:S(2)}) %collective-permute-start.5) | collective-permute-done | bytes 2097184 | tf_op jit(solution)/shard_map/ppermute | solution.py:19
  438.8 4.9 fusion.32
  447.0 8.0 %all-reduce = (f32[2,128]{1,0:T(2,128)S(1)}, f32[2,128]{1,0:T(2,128)S(1)}) all-reduce(f32[2,128]{1,0:T(2,128)S(1)} %multiply_reduce_fusion, f32[2,128]{1,0:T(2,128)S(1)} %multiply_reduce_fusion.1), channel_id=1, replica_groups=mesh['pair'=32,'row'=4] {'row'}, use_global_device_ids=true, to_apply=%region_22.23 | all-reduce | flops 512 | bytes 4096 | tf_op jit(solution)/shard_map/psum | solution.py:70
  455.0 28.5 %all-reduce.15.cloned.1.call-done = f32[2,128,128]{1,2,0:T(8,128)} async-done(((f32[2,128,128]{1,2,0:T(8,128)}), f32[2,128,128]{1,2,0:T(8,128)}) %all-reduce.15.cloned.1.call-update) | async-done | bytes 131088 | tf_op jit(solution)/shard_map/psum | solution.py:70
  506.3 11.0 %fusion.16 = f32[2,256,4096]{2,1,0:T(8,128)} fusion(f32[2,256,256]{1,2,0:T(8,128)S(1)} %fusion.38, f32[4096,1,128]{0,2,1:T(8,128)S(1)} %copy-done.20, f32[4096,1,128]{0,2,1:T(8,128)S(1)} %get-tuple-element.25, f32[4096,1,128]{0,2,1:T(8,128)S(1)} %copy-done.6, f32[4096,1,128]{0,2,1:T(8,128)S(1)} %copy-done.17), kind=kOutput, calls=%fused_computation.16 | convolution fusion | flops 6448742400 | bytes 17301504 | tf_op jit(solution)/shard_map/mpa,pab->mpb/dot_general | solution.py:74
  517.3 8.9 %copy.245 = f32[4096,512]{1,0:T(8,128)} copy(f32[4096,512]{0,1:T(8,128)} %bitcast.250) | data formatting | bytes 16777216 | tf_op jit(solution)/shard_map/reshape | solution.py:81
  (200 shorter events, 149.8 us)
Async XLA Ops:
  6.5 59.4 %all-reduce.9.cloned.1.call-start = ((), (), s32[]{:S(2)}) async-start(), calls=%async_computation | async-start | bytes 262144 | tf_op jit(solution)/shard_map/psum | solution.py:70
  23.5 187.1 %all-reduce.11.cloned.1.call-start = ((), (), s32[]{:S(2)}) async-start(), calls=%async_computation.1 | async-start | bytes 262144 | tf_op jit(solution)/shard_map/psum | solution.py:70
  80.6 8.7 %slice-start = ((s8[8388608]{0:T(1024)(128)(4,1)}), s8[4194304]{0:T(1024)(128)(4,1)S(1)}, s32[]{:S(2)}) async-start(s8[8388608]{0:T(1024)(128)(4,1)} %bitcast.247), calls=%async_computation.4 | async-start | bytes 8388608
  84.8 4.6 slice-start.1
  98.2 5.3 copy-start
  103.4 50.1 %collective-permute-start = (f32[4096,128]{0,1:T(8,128)}, f32[4096,128]{0,1:T(8,128)}, u32[]{:S(2)}, u32[]{:S(2)}) collective-permute-start(f32[4096,128]{0,1:T(8,128)} %get-tuple-element.35), channel_id=1, source_target_pairs={{0,4},{4,8},{8,12},{12,16},{16,20},{20,24},{24,28},{28,32},{32,36}... | collective-permute-start | bytes 6291464 | tf_op jit(solution)/shard_map/ppermute | solution.py:19
  105.9 54.0 %collective-permute-start.1 = (f32[4096,128]{0,1:T(8,128)}, f32[4096,128]{0,1:T(8,128)}, u32[]{:S(2)}, u32[]{:S(2)}) collective-permute-start(f32[4096,128]{0,1:T(8,128)} %get-tuple-element.36), channel_id=1, source_target_pairs={{4,0},{8,4},{12,8},{16,12},{20,16},{24,20},{28,24},{32,28},{36,32}... | collective-permute-start | bytes 6291464 | tf_op jit(solution)/shard_map/ppermute | solution.py:19
  109.4 56.5 %copy-start.1 = (f32[4096,1,128]{0,2,1:T(8,128)S(1)}, f32[4096,1,128]{0,2,1:T(8,128)}, u32[]{:S(2)}) copy-start(f32[4096,1,128]{0,2,1:T(8,128)} %get-tuple-element.38) | copy-start | bytes 6291460
  170.9 176.2 %all-reduce.13.cloned.1.call-start = ((), (), s32[]{:S(2)}) async-start(), calls=%async_computation.2 | async-start | bytes 262144 | tf_op jit(solution)/shard_map/psum | solution.py:70
  229.4 4.3 copy-start.10
  231.2 2.5 copy-start.2
  243.5 56.8 %copy-start.3 = (f32[4096,1,128]{0,2,1:T(8,128)}, f32[4096,1,128]{0,2,1:T(8,128)S(1)}, u32[]{:S(2)}) copy-start(f32[4096,1,128]{0,2,1:T(8,128)S(1)} %get-tuple-element.32) | copy-start | bytes 6291460
  243.5 49.8 %collective-permute-start.2 = (f32[4096,128]{0,1:T(8,128)S(1)}, f32[4096,128]{0,1:T(8,128)S(1)}, u32[]{:S(2)}, u32[]{:S(2)}) collective-permute-start(f32[4096,128]{0,1:T(8,128)S(1)} %get-tuple-element.29), channel_id=1, source_target_pairs={{0,4},{4,8},{8,12},{12,16},{16,20},{20,24},{24,28},{28,32},{32,36}... | collective-permute-start | bytes 6291464 | tf_op jit(solution)/shard_map/ppermute | solution.py:19
  246.0 53.7 %collective-permute-start.3 = (f32[4096,128]{0,1:T(8,128)S(1)}, f32[4096,128]{0,1:T(8,128)S(1)}, u32[]{:S(2)}, u32[]{:S(2)}) collective-permute-start(f32[4096,128]{0,1:T(8,128)S(1)} %get-tuple-element.30), channel_id=1, source_target_pairs={{4,0},{8,4},{12,8},{16,12},{20,16},{24,20},{28,24},{32,28},{36,32}... | collective-permute-start | bytes 6291464 | tf_op jit(solution)/shard_map/ppermute | solution.py:19
  307.3 176.2 %all-reduce.15.cloned.1.call-start = ((), (), s32[]{:S(2)}) async-start(), calls=%async_computation.3 | async-start | bytes 262144 | tf_op jit(solution)/shard_map/psum | solution.py:70
  307.4 2.9 copy-start.14
  365.8 4.3 copy-start.15
  379.9 56.8 %copy-start.5 = (f32[4096,1,128]{0,2,1:T(8,128)}, f32[4096,1,128]{0,2,1:T(8,128)S(1)}, u32[]{:S(2)}) copy-start(f32[4096,1,128]{0,2,1:T(8,128)S(1)} %get-tuple-element.26) | copy-start | bytes 6291460
  379.9 49.8 %collective-permute-start.4 = (f32[4096,128]{0,1:T(8,128)S(1)}, f32[4096,128]{0,1:T(8,128)S(1)}, u32[]{:S(2)}, u32[]{:S(2)}) collective-permute-start(f32[4096,128]{0,1:T(8,128)S(1)} %get-tuple-element.23), channel_id=1, source_target_pairs={{0,4},{4,8},{8,12},{12,16},{16,20},{20,24},{24,28},{28,32},{32,36}... | collective-permute-start | bytes 6291464 | tf_op jit(solution)/shard_map/ppermute | solution.py:19
  382.4 53.7 %collective-permute-start.5 = (f32[4096,128]{0,1:T(8,128)S(1)}, f32[4096,128]{0,1:T(8,128)S(1)}, u32[]{:S(2)}, u32[]{:S(2)}) collective-permute-start(f32[4096,128]{0,1:T(8,128)S(1)} %get-tuple-element.24), channel_id=1, source_target_pairs={{4,0},{8,4},{12,8},{16,12},{20,16},{24,20},{28,24},{32,28},{36,32}... | collective-permute-start | bytes 6291464 | tf_op jit(solution)/shard_map/ppermute | solution.py:19
  443.7 2.9 copy-start.19
  501.6 4.7 copy-start.20
  503.3 2.9 copy-start.6
  503.4 2.9 copy-start.17
  (10 other events, 19.2 us)
Sparse Core Ops, SparseCore 0:
  23.6 42.2 all-reduce.8
  171.0 39.6 all-reduce.10
  307.4 39.6 all-reduce.12
  443.8 39.6 all-reduce.14
where the time goes:
time: 540 us; the launch traced here: 533 us
  waiting for transfers between devices  253 us (47%)
  matrix products  146 us (27%)
  blocking collectives  35.1 us (6%)
  local copies, waits for them, and re-layouts  33.6 us (6%)
  other arithmetic  32.9 us (6%)
  starting transfers between devices  17.6 us (3%)
  between operations  15 us (3%)
    ppermute x6, waiting for transfers between devices, shifted(): lax.ppermute(value, axis, [(source, source + steps) for source in range(i...  151 us
    psum x4, waiting for transfers between devices, per_device(): gram, norm_top, norm_bottom = lax.psum((gram, norm_top, norm_bottom), 'row')  102 us
    dot_general x48, matrix products, polar_from(): matrix = 1.5 * matrix - 0.5 * jnp.dot(matrix, inner, precision=HIGH)  42.7 us
    dot_general x48, matrix products, polar_from(): inner = jnp.dot(matrix.T, matrix, precision=HIGH)  42.6 us
    dot_general x4, matrix products, per_device(): joined = jnp.einsum('mpa,pab->mpb', joined, polar, precision=HIGH)  37.4 us
    psum x4, blocking collectives, per_device(): gram, norm_top, norm_bottom = lax.psum((gram, norm_top, norm_bottom), 'row')  35.1 us
    dot_general x4, matrix products, per_device(): gram = jnp.einsum('mpi,mpj->pij', top, bottom, precision=HIGH)  22.9 us
    unnamed x51, local copies, waits for them, and re-layouts  22.7 us
  transfers between devices with their start and end apart: 10, of which 10 were waited for; matrix products, arithmetic and copies ran while one was open for 5% of the time, Pallas kernels for 0%

commit v1 on v0

v1 whole, which is shorter than its diff:
```python
import functools
import jax
import jax.numpy as jnp
from jax import lax
from jax.experimental import pallas as pl
from jax.experimental.pallas import tpu as pltpu
from jax.sharding import PartitionSpec as P

B = 128
STEPS = 4
ITERS = 12
EPS = 1e-06
DAMPING = 0.04
CHUNKS = 1
TILE = 512
GROWS = 136
F32 = jnp.float32
BF16 = jnp.bfloat16
PARAMS = pltpu.CompilerParams(vmem_limit_bytes=40 * 1024 * 1024)
NN = (((1,), (0,)), ((), ()))
NT = (((1,), (1,)), ((), ()))
TN = (((0,), (0,)), ((), ()))


def halves(value):
    high = value.astype(BF16)
    return high, (value - high.astype(F32)).astype(BF16)


def dot(a, b, dims=NN):
    return lax.dot_general(a, b, dims, preferred_element_type=F32)


def dot3(a, b, dims=NN):
    return dot(a[0], b[0], dims) + (dot(a[0], b[1], dims) + dot(a[1], b[0], dims))


def beside(a, b):
    return jnp.concatenate([a, b], axis=1)


def add_gram(g_ref, pair, top, bottom):
    product = dot(beside(*halves(top)), beside(*halves(bottom)), TN)
    g_ref[pair, :B, :] += (product[:B, :B] + product[B:, B:]) + (product[:B, B:] + product[B:, :B])
    g_ref[pair, B : B + 1, :] += jnp.sum(top * top, axis=0, keepdims=True)
    g_ref[pair, B + 1 : B + 2, :] += jnp.sum(bottom * bottom, axis=0, keepdims=True)


def gram_first_kernel(x_ref, g_ref):
    @pl.when(pl.program_id(0) == 0)
    def _():
        g_ref[...] = jnp.zeros_like(g_ref)

    for pair in range(2):
        base = 2 * B * pair
        add_gram(g_ref, pair, x_ref[:, base : base + B], x_ref[:, base + B : base + 2 * B])


def gram_first(x):
    rows = x.shape[0]
    tile = min(TILE, rows)
    return pl.pallas_call(
        gram_first_kernel,
        grid=(rows // tile,),
        in_specs=[pl.BlockSpec((tile, 4 * B), lambda i: (i, 0))],
        out_specs=pl.BlockSpec((2, GROWS, B), lambda i: (0, 0, 0)),
        out_shape=jax.ShapeDtypeStruct((2, GROWS, B), F32),
        compiler_params=PARAMS,
        name="gram_first",
    )(x)


def gram_next_kernel(rebuild, flag_ref, first_ref, last_ref, b0_ref, t1_ref, in_top_ref, in_bottom_ref, *rest):
    if rebuild:
        prev_left_ref, prev_right_ref, q_top_ref, q_bottom_ref, g_in_ref, g_ref, t0_ref, b1_ref = rest
    else:
        g_in_ref, g_ref, t0_ref, b1_ref = rest

    @pl.when(pl.program_id(0) == 0)
    def _():
        g_ref[...] = g_in_ref[...]

    in_top, in_bottom = in_top_ref[...], in_bottom_ref[...]
    if rebuild:
        in_top = dot3(halves(beside(in_top, prev_left_ref[...])), halves(q_top_ref[...]))
        in_bottom = dot3(halves(beside(prev_right_ref[...], in_bottom)), halves(q_bottom_ref[...]))
    t0 = jnp.where(flag_ref[0] == 1, first_ref[...], in_top)
    b1 = jnp.where(flag_ref[1] == 1, last_ref[...], in_bottom)
    t0_ref[...] = t0
    b1_ref[...] = b1
    add_gram(g_ref, 0, t0, b0_ref[...])
    add_gram(g_ref, 1, t1_ref[...], b1)


def gram_next(flags, blocks, rebuilt, g_in):
    rows = blocks[0].shape[0]
    tile = min(TILE, rows)
    block = pl.BlockSpec((tile, B), lambda i: (i, 0))
    half = pl.BlockSpec((2 * B, B), lambda i: (0, 0))
    gram = pl.BlockSpec((2, GROWS, B), lambda i: (0, 0, 0))
    extra = [block, block, half, half] if rebuilt else []
    return pl.pallas_call(
        functools.partial(gram_next_kernel, bool(rebuilt)),
        grid=(rows // tile,),
        in_specs=[pl.BlockSpec(memory_space=pltpu.SMEM)] + [block] * 6 + extra + [gram],
        out_specs=[gram, block, block],
        out_shape=[jax.ShapeDtypeStruct((2, GROWS, B), F32)] + [jax.ShapeDtypeStruct((rows, B), F32)] * 2,
        compiler_params=PARAMS,
        name="gram_next",
    )(flags, *blocks, *rebuilt, g_in)


def polar_kernel(g0_ref, g1_ref, g2_ref, g3_ref, q_ref, right_ref, left_ref):
    total = (g0_ref[...] + g1_ref[...]) + (g2_ref[...] + g3_ref[...])
    eye = (lax.broadcasted_iota(jnp.int32, (B, B), 0) == lax.broadcasted_iota(jnp.int32, (B, B), 1)).astype(F32)
    chains = []
    for pair in range(2):
        gram = total[pair, :B]
        norm_top = jnp.transpose(jnp.broadcast_to(total[pair, B : B + 1], (B, B)))
        norm_bottom = jnp.broadcast_to(total[pair, B + 1 : B + 2], (B, B))
        differ = norm_top - norm_bottom
        both = norm_top + norm_bottom + EPS
        radius = jnp.sqrt(differ * differ + 4.0 * gram * gram)
        denominator = differ * differ + jnp.abs(differ) * radius + DAMPING * both * both
        coupling = -2.0 * gram * differ / denominator
        scale = lax.rsqrt(1.0 + jnp.sum(coupling * coupling, keepdims=True))
        chains.append(beside(eye, coupling) * scale)
        chains.append(beside(-jnp.transpose(coupling), eye) * scale)

    def iterate(_, chains):
        parts = [halves(chain) for chain in chains]
        inner = [halves(dot3(part, part, NT)) for part in parts]
        return tuple(1.5 * chain - 0.5 * dot3(m, part) for chain, m, part in zip(chains, inner, parts))

    chains = lax.fori_loop(0, ITERS, iterate, tuple(chains))
    for pair in range(2):
        q_ref[pair, :B, :] = chains[2 * pair]
        q_ref[pair, B:, :] = chains[2 * pair + 1]
    right_ref[:B, :] = chains[2][:, :B]
    right_ref[B:, :] = chains[3][:, :B]
    left_ref[:B, :] = chains[0][:, B:]
    left_ref[B:, :] = chains[1][:, B:]


def polar(grams):
    return pl.pallas_call(
        polar_kernel,
        out_shape=[
            jax.ShapeDtypeStruct((2, 2 * B, 2 * B), F32),
            jax.ShapeDtypeStruct((2 * B, B), F32),
            jax.ShapeDtypeStruct((2 * B, B), F32),
        ],
        compiler_params=PARAMS,
        name="polar",
    )(*grams)


def rotate_kernel(whole, last, flag_ref, *refs):
    if whole:
        x_ref, q_ref, *outs = refs
        pairs = [x_ref[:, : 2 * B], x_ref[:, 2 * B :]]
    else:
        t0_ref, b0_ref, t1_ref, b1_ref, q_ref, *outs = refs
        pairs = [beside(t0_ref[...], b0_ref[...]), beside(t1_ref[...], b1_ref[...])]
    turned = [dot3(halves(pairs[k]), halves(q_ref[k])) for k in range(2)]
    if last:
        outs[0][:, : 2 * B] = turned[0]
        outs[0][:, 2 * B :] = turned[1]
        return
    right_ref, left_ref, t1n_ref, b0n_ref = outs
    first = flag_ref[0] == 1
    t0, b0 = turned[0][:, :B], turned[0][:, B:]
    right_ref[...] = turned[1][:, :B]
    left_ref[...] = jnp.where(first, t0, b0)
    t1n_ref[...] = jnp.where(first, b0, t0)
    b0n_ref[...] = turned[1][:, B:]


def rotate(flags, blocks, q, last=False, rows=None, start=0):
    whole = len(blocks) == 1
    rows = rows or blocks[0].shape[0]
    tile = min(TILE, rows)
    offset = start // tile
    block = pl.BlockSpec((tile, B), lambda i: (i, 0))
    wide = pl.BlockSpec((tile, 4 * B), lambda i: (i + offset, 0))
    full = pl.BlockSpec((2, 2 * B, 2 * B), lambda i: (0, 0, 0))
    if last:
        out_specs, out_shape = wide, jax.ShapeDtypeStruct((rows, 4 * B), F32)
    else:
        out_specs, out_shape = [block] * 4, [jax.ShapeDtypeStruct((rows, B), F32)] * 4
    return pl.pallas_call(
        functools.partial(rotate_kernel, whole, last),
        grid=(rows // tile,),
        in_specs=[pl.BlockSpec(memory_space=pltpu.SMEM)] + ([wide] if whole else [block] * 4) + [full],
        out_specs=out_specs,
        out_shape=out_shape,
        compiler_params=PARAMS,
        name="rotate",
    )(flags, *blocks, q)


def shifted(value, steps):
    count = lax.axis_size("pair")
    initial, last = (max(0, -steps), min(count, count - steps))
    return lax.ppermute(value, "pair", [(source, source + steps) for source in range(initial, last)])


def row_terms(value):
    count = lax.axis_size("row")
    return [value] + [lax.ppermute(value, "row", [(i, i ^ k) for i in range(count)]) for k in range(1, count)]


def after(values, done):
    return lax.optimization_barrier((values, done))


def per_device(factor):
    position = lax.axis_index("pair")
    flags = jnp.stack([position == 0, position == lax.axis_size("pair") - 1]).astype(jnp.int32)
    zero = jnp.zeros((2, GROWS, B), F32)

    q, _, _ = polar(row_terms(gram_first(factor)))
    right, left, t1, b0 = rotate(flags, [factor], q)
    arrived = (shifted(right, 1), shifted(left, -1))
    (t1, b0), arrived = after((t1, b0), arrived)
    ahead = (shifted(t1, 1), shifted(b0, -1))
    previous = (left, right)
    rebuilt = ()
    for step in range(1, STEPS):
        g, t0, b1 = gram_next(flags, (left, right, b0, t1, *arrived), rebuilt, zero)
        q, q_right, q_left = polar(row_terms(g))
        if step == STEPS - 1:
            return rotate(flags, [t0, b0, t1, b1], q, last=True)
        q_top, q_bottom = shifted(q_right, 1), shifted(q_left, -1)
        older = previous
        right, left, t1, b0 = rotate(flags, [t0, b0, t1, b1], q)
        previous = (left, right)
        rebuilt = (*older, q_top, q_bottom)
        arrived = ahead
        if step < STEPS - 2:
            (t1, b0), arrived = after((t1, b0), arrived)
            ahead = (shifted(t1, 1), shifted(b0, -1))


def solution(mesh):
    placed = (P("row", "pair"),)
    return jax.shard_map(
        per_device, mesh=mesh, in_specs=placed, out_specs=P("row", "pair"), check_vma=False
    )
```

time: 540 us -> 306 us (0.57)
  the two profiles are of different devices: /device:TPU:30 before, /device:TPU:63 now
where the time goes in v1:
time: 306 us; the launch traced here: 305 us
  waiting for transfers between devices  156 us (51%)
  Pallas kernels  94.8 us (31%)
  starting transfers between devices  46.1 us (15%)
  local copies, waits for them, and re-layouts  7.44 us (2%)
    ppermute x10, waiting for transfers between devices, shifted(): lax.ppermute(value, 'pair', [(source, source + steps) for source in range...  84.6 us
    ppermute x12, waiting for transfers between devices, row_terms(): lax.ppermute(value, 'row', [(i, i ^ k) for i in range(count)])  71.8 us
    pallas_call x4, Pallas kernels, polar(): pl.pallas_call(polar_kernel, out_shape=[jax.ShapeDtypeStruct((2, 2 * B, 2...  33.2 us
    pallas_call x4, Pallas kernels, rotate(): pl.pallas_call(functools.partial(rotate_kernel, whole, last), grid=(rows...  32.2 us
    ppermute x10, starting transfers between devices, shifted(): lax.ppermute(value, 'pair', [(source, source + steps) for source in range...  28.8 us
    pallas_call x3, Pallas kernels, gram_next(): pl.pallas_call(functools.partial(gram_next_kernel, bool(rebuilt)), grid=(...  26 us
    ppermute x12, starting transfers between devices, row_terms(): lax.ppermute(value, 'row', [(i, i ^ k) for i in range(count)])  17.3 us
    unnamed x26, local copies, waits for them, and re-layouts  7.43 us
  transfers between devices with their start and end apart: 22, of which 12 were waited for; matrix products, arithmetic and copies ran while one was open for 0% of the time, Pallas kernels for 16%

profile of v1, /device:TPU:63, one launch (start us, length us, event | category | flops | bytes accessed | tf_op | source)
XLA Modules:
  0.0 305.1 jit_solution(11808921250865628421)
XLA Ops:
  10.8 3.4 %collective-permute-done.1.g2_ref = f32[2,136,128]{2,1,0:T(8,128)S(1)} collective-permute-done((f32[2,136,128]{2,1,0:T(8,128)S(1)}, f32[2,136,128]{2,1,0:T(8,128)S(1)}, u32[]{:S(2)}, u32[]{:S(2)}) %collective-permute-start.1) | collective-permute-done | bytes 139296 | tf_op jit(solution)/shard_map/ppermute | solution.py:210
  17.4 8.6 %polar.4 = (f32[2,256,256]{2,1,0:T(8,128)S(1)}, f32[256,128]{1,0:T(8,128)}, f32[256,128]{1,0:T(8,128)}) custom-call(f32[2,136,128]{2,1,0:T(8,128)S(1)} %gram_first.1.g0_ref, f32[2,136,128]{2,1,0:T(8,128)S(1)} %collective-permute-done.g1_ref, f32[2,136,128]{2,1,0:T(8,128)S(1)} %collective-permute-done.1.g2_ref, f32[2,136,128]{2,1,0:T(8,128)S(1)} %collective-permute-done.2.g3_ref), custom_call_target="tpu_custom_call" | custom-call | tf_op jit(solution)/shard_map/polar/pallas_call | solution.py:146
  26.0 9.6 %rotate.4 = (f32[4096,128]{1,0:T(8,128)S(1)}, f32[4096,128]{1,0:T(8,128)S(1)}, f32[4096,128]{1,0:T(8,128)}, f32[4096,128]{1,0:T(8,128)}) custom-call(s32[2]{0:T(128)S(1)} %add_convert_fusion.flag_ref, f32[4096,512]{1,0:T(8,128)} %refs_0_.1, f32[2,256,256]{2,1,0:T(8,128)S(1)} %get-tuple-element.42.refs_1_), custom_call_target="tpu_custom_call" | custom-call | tf_op jit(solution)/shard_map/rotate/pallas_call | solution.py:191
  36.9 4.1 %collective-permute-start.4 = (f32[4096,128]{1,0:T(8,128)S(1)}, f32[4096,128]{1,0:T(8,128)S(1)}, u32[]{:S(2)}, u32[]{:S(2)}) collective-permute-start(f32[4096,128]{1,0:T(8,128)S(1)} %get-tuple-element.43.first_ref.rest_0_), channel_id=1, source_target_pairs={{4,0},{8,4},{12,8},{16,12},{20,16},{24,20},{28,24},{32,28},{36,32}... | collective-permute-start | bytes 6291464 | tf_op jit(solution)/shard_map/ppermute | solution.py:205
  41.0 43.3 %collective-permute-done.3.in_top_ref = f32[4096,128]{1,0:T(8,128)S(1)} collective-permute-done((f32[4096,128]{1,0:T(8,128)S(1)}, f32[4096,128]{1,0:T(8,128)S(1)}, u32[]{:S(2)}, u32[]{:S(2)}) %collective-permute-start.3) | collective-permute-done | bytes 2097184 | tf_op jit(solution)/shard_map/ppermute | solution.py:205
  86.5 4.9 %collective-permute-start.9 = (f32[4096,128]{1,0:T(8,128)}, f32[4096,128]{1,0:T(8,128)S(1)}, u32[]{:S(2)}, u32[]{:S(2)}) collective-permute-start(f32[4096,128]{1,0:T(8,128)} %get-tuple-element.47.b0_ref.refs_1_), channel_id=1, source_target_pairs={{4,0},{8,4},{12,8},{16,12},{20,16},{24,20},{28,24},{32,28},{36,32}... | collective-permute-start | bytes 6291464 | tf_op jit(solution)/shard_map/ppermute | solution.py:205
  91.4 7.4 %gram_next.3 = (f32[2,136,128]{2,1,0:T(8,128)S(1)}, f32[4096,128]{1,0:T(8,128)S(1)}, f32[4096,128]{1,0:T(8,128)S(1)}) custom-call(s32[2]{0:T(128)S(1)} %add_convert_fusion.flag_ref, f32[4096,128]{1,0:T(8,128)S(1)} %get-tuple-element.43.first_ref.rest_0_, f32[4096,128]{1,0:T(8,128)S(1)} %get-tuple-element.44.last_ref.rest_1_, ...), custom_call_target="tpu_custom_call" | custom-call | tf_op jit(solution)/shard_map/gram_next/pallas_call | solution.py:102
  105.1 46.3 %collective-permute-done.6.g2_ref = f32[2,136,128]{2,1,0:T(8,128)S(1)} collective-permute-done((f32[2,136,128]{2,1,0:T(8,128)S(1)}, f32[2,136,128]{2,1,0:T(8,128)S(1)}, u32[]{:S(2)}, u32[]{:S(2)}) %collective-permute-start.6) | collective-permute-done | bytes 139296 | tf_op jit(solution)/shard_map/ppermute | solution.py:210
  154.4 8.0 %polar.5 = (f32[2,256,256]{2,1,0:T(8,128)S(1)}, f32[256,128]{1,0:T(8,128)S(1)}, f32[256,128]{1,0:T(8,128)S(1)}) custom-call(f32[2,136,128]{2,1,0:T(8,128)S(1)} %get-tuple-element.53.g0_ref, f32[2,136,128]{2,1,0:T(8,128)S(1)} %collective-permute-done.5.g1_ref, f32[2,136,128]{2,1,0:T(8,128)S(1)} %collective-permute-done.6.g2_ref, ...), custom_call_target="tpu_custom_call" | custom-call | tf_op jit(solution)/shard_map/polar/pallas_call | solution.py:146
  162.4 7.8 %rotate.5 = (f32[4096,128]{1,0:T(8,128)S(1)}, f32[4096,128]{1,0:T(8,128)S(1)}, f32[4096,128]{1,0:T(8,128)S(1)}, f32[4096,128]{1,0:T(8,128)S(1)}) custom-call(s32[2]{0:T(128)S(1)} %add_convert_fusion.flag_ref, f32[4096,128]{1,0:T(8,128)S(1)} %get-tuple-element.51.refs_0_, f32[4096,128]{1,0:T(8,128)} %get-tuple-element.47.b0_ref.refs_1_, ...), custom_call_target="tpu_custom_call" | custom-call | tf_op jit(solution)/shard_map/rotate/pallas_call | solution.py:191
  171.5 5.4 %collective-permute-start.16 = (f32[4096,128]{1,0:T(8,128)S(1)}, f32[4096,128]{1,0:T(8,128)}, u32[]{:S(2)}, u32[]{:S(2)}) collective-permute-start(f32[4096,128]{1,0:T(8,128)S(1)} %get-tuple-element.59.b0_ref.refs_1_), channel_id=1, source_target_pairs={{4,0},{8,4},{12,8},{16,12},{20,16},{24,20},{28,24},{32,28},{36,32}... | collective-permute-start | bytes 6291464 | tf_op jit(solution)/shard_map/ppermute | solution.py:205
  178.2 4.0 %collective-permute-start.11 = (f32[256,128]{1,0:T(8,128)S(1)}, f32[256,128]{1,0:T(8,128)S(1)}, u32[]{:S(2)}, u32[]{:S(2)}) collective-permute-start(f32[256,128]{1,0:T(8,128)S(1)} %get-tuple-element.64), channel_id=1, source_target_pairs={{4,0},{8,4},{12,8},{16,12},{20,16},{24,20},{28,24},{32,28},{36,32}... | collective-permute-start | bytes 393224 | tf_op jit(solution)/shard_map/ppermute | solution.py:205
  182.2 39.6 %collective-permute-done.10.rest_2_ = f32[256,128]{1,0:T(8,128)S(1)} collective-permute-done((f32[256,128]{1,0:T(8,128)S(1)}, f32[256,128]{1,0:T(8,128)S(1)}, u32[]{:S(2)}, u32[]{:S(2)}) %collective-permute-start.10) | collective-permute-done | bytes 131104 | tf_op jit(solution)/shard_map/ppermute | solution.py:205
  222.6 9.3 %gram_next.4 = (f32[2,136,128]{2,1,0:T(8,128)S(1)}, f32[4096,128]{1,0:T(8,128)S(1)}, f32[4096,128]{1,0:T(8,128)S(1)}) custom-call(s32[2]{0:T(128)S(1)} %add_convert_fusion.flag_ref, f32[4096,128]{1,0:T(8,128)S(1)} %get-tuple-element.55.first_ref.rest_0_, f32[4096,128]{1,0:T(8,128)S(1)} %get-tuple-element.56.last_ref.rest_1_, ...), custom_call_target="tpu_custom_call" | custom-call | tf_op jit(solution)/shard_map/gram_next/pallas_call | solution.py:102
  238.0 3.7 %collective-permute-done.13.g2_ref = f32[2,136,128]{2,1,0:T(8,128)S(1)} collective-permute-done((f32[2,136,128]{2,1,0:T(8,128)S(1)}, f32[2,136,128]{2,1,0:T(8,128)S(1)}, u32[]{:S(2)}, u32[]{:S(2)}) %collective-permute-start.13) | collective-permute-done | bytes 139296 | tf_op jit(solution)/shard_map/ppermute | solution.py:210
  241.7 5.9 %collective-permute-done.14.g3_ref = f32[2,136,128]{2,1,0:T(8,128)S(1)} collective-permute-done((f32[2,136,128]{2,1,0:T(8,128)S(1)}, f32[2,136,128]{2,1,0:T(8,128)S(1)}, u32[]{:S(2)}, u32[]{:S(2)}) %collective-permute-start.14) | collective-permute-done | bytes 139296 | tf_op jit(solution)/shard_map/ppermute | solution.py:210
  247.6 8.0 %polar.6 = (f32[2,256,256]{2,1,0:T(8,128)S(1)}, f32[256,128]{1,0:T(8,128)S(1)}, f32[256,128]{1,0:T(8,128)S(1)}) custom-call(f32[2,136,128]{2,1,0:T(8,128)S(1)} %get-tuple-element.67.g0_ref, f32[2,136,128]{2,1,0:T(8,128)S(1)} %collective-permute-done.12.g1_ref, f32[2,136,128]{2,1,0:T(8,128)S(1)} %collective-permute-done.13.g2_ref, ...), custom_call_target="tpu_custom_call" | custom-call | tf_op jit(solution)/shard_map/polar/pallas_call | solution.py:146
  256.9 4.0 %collective-permute-start.18 = (f32[256,128]{1,0:T(8,128)S(1)}, f32[256,128]{1,0:T(8,128)S(1)}, u32[]{:S(2)}, u32[]{:S(2)}) collective-permute-start(f32[256,128]{1,0:T(8,128)S(1)} %get-tuple-element.74), channel_id=1, source_target_pairs={{4,0},{8,4},{12,8},{16,12},{20,16},{24,20},{28,24},{32,28},{36,32}... | collective-permute-start | bytes 393224 | tf_op jit(solution)/shard_map/ppermute | solution.py:205
  260.9 7.4 %rotate.6 = (f32[4096,128]{1,0:T(8,128)S(1)}, f32[4096,128]{1,0:T(8,128)S(1)}, f32[4096,128]{1,0:T(8,128)S(1)}, f32[4096,128]{1,0:T(8,128)S(1)}) custom-call(s32[2]{0:T(128)S(1)} %add_convert_fusion.flag_ref, f32[4096,128]{1,0:T(8,128)S(1)} %get-tuple-element.65.refs_0_, f32[4096,128]{1,0:T(8,128)S(1)} %get-tuple-element.59.b0_ref.refs_1_, ...), custom_call_target="tpu_custom_call" | custom-call | tf_op jit(solution)/shard_map/rotate/pallas_call | solution.py:191
  269.6 9.3 %gram_next.5 = (f32[2,136,128]{2,1,0:T(8,128)S(1)}, f32[4096,128]{1,0:T(8,128)S(1)}, f32[4096,128]{1,0:T(8,128)S(1)}) custom-call(s32[2]{0:T(128)S(1)} %add_convert_fusion.flag_ref, f32[4096,128]{1,0:T(8,128)S(1)} %get-tuple-element.69.first_ref, f32[4096,128]{1,0:T(8,128)S(1)} %get-tuple-element.70.last_ref, ...), custom_call_target="tpu_custom_call" | custom-call | tf_op jit(solution)/shard_map/gram_next/pallas_call | solution.py:102
  279.1 3.5 %collective-permute-start.21 = (f32[2,136,128]{2,1,0:T(8,128)S(1)}, f32[2,136,128]{2,1,0:T(8,128)S(1)}, u32[]{:S(2)}, u32[]{:S(2)}) collective-permute-start(f32[2,136,128]{2,1,0:T(8,128)S(1)} %get-tuple-element.77.g0_ref), channel_id=1, source_target_pairs={{0,3},{1,2},{2,1},{3,0},{4,7},{5,6},{6,5},{7,4},{8,11},{9,10},{10,... | collective-permute-start | bytes 417800 | tf_op jit(solution)/shard_map/ppermute | solution.py:210
  285.5 3.5 %collective-permute-done.21.g3_ref = f32[2,136,128]{2,1,0:T(8,128)S(1)} collective-permute-done((f32[2,136,128]{2,1,0:T(8,128)S(1)}, f32[2,136,128]{2,1,0:T(8,128)S(1)}, u32[]{:S(2)}, u32[]{:S(2)}) %collective-permute-start.21) | collective-permute-done | bytes 139296 | tf_op jit(solution)/shard_map/ppermute | solution.py:210
  289.0 8.6 %polar.7 = (f32[2,256,256]{2,1,0:T(8,128)S(1)}, f32[256,128]{1,0:T(8,128)}, f32[256,128]{1,0:T(8,128)}) custom-call(f32[2,136,128]{2,1,0:T(8,128)S(1)} %get-tuple-element.77.g0_ref, f32[2,136,128]{2,1,0:T(8,128)S(1)} %collective-permute-done.19.g1_ref, f32[2,136,128]{2,1,0:T(8,128)S(1)} %collective-permute-done.20.g2_ref, ...), custom_call_target="tpu_custom_call" | custom-call | tf_op jit(solution)/shard_map/polar/pallas_call | solution.py:146
  297.6 7.5 %rotate.7 = f32[4096,512]{1,0:T(8,128)} custom-call(s32[2]{0:T(128)S(1)} %add_convert_fusion.flag_ref, f32[4096,128]{1,0:T(8,128)S(1)} %get-tuple-element.75.refs_0_, f32[4096,128]{1,0:T(8,128)S(1)} %get-tuple-element.71.b0_ref.refs_1_, f32[4096,128]{1,0:T(8,128)S(1)} %get-tuple-element.72.t1_ref.refs_2_, f32[4096,128]{1,0:T(8,128)S(1)} %get-tuple-element.76.refs_3_, ...), custom_call_target="tpu_custom_call" | custom-call | tf_op jit(solution)/shard_map/rotate/pallas_call | solution.py:191
  (60 shorter events, 41.8 us)
Async XLA Ops:
  6.8 4.1 %collective-permute-start = (f32[2,136,128]{2,1,0:T(8,128)S(1)}, f32[2,136,128]{2,1,0:T(8,128)S(1)}, u32[]{:S(2)}, u32[]{:S(2)}) collective-permute-start(f32[2,136,128]{2,1,0:T(8,128)S(1)} %gram_first.1.g0_ref), channel_id=1, source_target_pairs={{0,1},{1,0},{2,3},{3,2},{4,5},{5,4},{6,7},{7,6},{8,9},{9,8},{10,11... | collective-permute-start | bytes 417800 | tf_op jit(solution)/shard_map/ppermute | solution.py:210
  7.5 6.7 %collective-permute-start.1 = (f32[2,136,128]{2,1,0:T(8,128)S(1)}, f32[2,136,128]{2,1,0:T(8,128)S(1)}, u32[]{:S(2)}, u32[]{:S(2)}) collective-permute-start(f32[2,136,128]{2,1,0:T(8,128)S(1)} %gram_first.1.g0_ref), channel_id=1, source_target_pairs={{0,2},{1,3},{2,0},{3,1},{4,6},{5,7},{6,4},{7,5},{8,10},{9,11},{10,... | collective-permute-start | bytes 417800 | tf_op jit(solution)/shard_map/ppermute | solution.py:210
  10.2 7.2 %collective-permute-start.2 = (f32[2,136,128]{2,1,0:T(8,128)S(1)}, f32[2,136,128]{2,1,0:T(8,128)S(1)}, u32[]{:S(2)}, u32[]{:S(2)}) collective-permute-start(f32[2,136,128]{2,1,0:T(8,128)S(1)} %gram_first.1.g0_ref), channel_id=1, source_target_pairs={{0,3},{1,2},{2,1},{3,0},{4,7},{5,6},{6,5},{7,4},{8,11},{9,10},{10,... | collective-permute-start | bytes 417800 | tf_op jit(solution)/shard_map/ppermute | solution.py:210
  35.6 63.1 %copy-start.4 = (f32[4096,128]{1,0:T(8,128)}, f32[4096,128]{1,0:T(8,128)S(1)}, u32[]{:S(2)}) copy-start(f32[4096,128]{1,0:T(8,128)S(1)} %get-tuple-element.44.last_ref.rest_1_) | copy-start | bytes 6291460
  35.6 63.1 %copy-start.5 = (f32[4096,128]{1,0:T(8,128)}, f32[4096,128]{1,0:T(8,128)S(1)}, u32[]{:S(2)}) copy-start(f32[4096,128]{1,0:T(8,128)S(1)} %get-tuple-element.43.first_ref.rest_0_) | copy-start | bytes 6291460
  35.6 48.7 %collective-permute-start.3 = (f32[4096,128]{1,0:T(8,128)S(1)}, f32[4096,128]{1,0:T(8,128)S(1)}, u32[]{:S(2)}, u32[]{:S(2)}) collective-permute-start(f32[4096,128]{1,0:T(8,128)S(1)} %get-tuple-element.44.last_ref.rest_1_), channel_id=1, source_target_pairs={{0,4},{4,8},{8,12},{12,16},{16,20},{20,24},{24,28},{28,32},{32,36}... | collective-permute-start | bytes 6291464 | tf_op jit(solution)/shard_map/ppermute | solution.py:205
  36.9 48.3 %collective-permute-start.4 = (f32[4096,128]{1,0:T(8,128)S(1)}, f32[4096,128]{1,0:T(8,128)S(1)}, u32[]{:S(2)}, u32[]{:S(2)}) collective-permute-start(f32[4096,128]{1,0:T(8,128)S(1)} %get-tuple-element.43.first_ref.rest_0_), channel_id=1, source_target_pairs={{4,0},{8,4},{12,8},{16,12},{20,16},{24,20},{28,24},{32,28},{36,32}... | collective-permute-start | bytes 6291464 | tf_op jit(solution)/shard_map/ppermute | solution.py:205
  85.2 85.0 %collective-permute-start.8 = (f32[4096,128]{1,0:T(8,128)}, f32[4096,128]{1,0:T(8,128)S(1)}, u32[]{:S(2)}, u32[]{:S(2)}) collective-permute-start(f32[4096,128]{1,0:T(8,128)} %get-tuple-element.48.t1_ref.refs_2_), channel_id=1, source_target_pairs={{0,4},{4,8},{8,12},{12,16},{16,20},{20,24},{24,28},{28,32},{32,36}... | collective-permute-start | bytes 6291464 | tf_op jit(solution)/shard_map/ppermute | solution.py:205
  86.5 83.8 %collective-permute-start.9 = (f32[4096,128]{1,0:T(8,128)}, f32[4096,128]{1,0:T(8,128)S(1)}, u32[]{:S(2)}, u32[]{:S(2)}) collective-permute-start(f32[4096,128]{1,0:T(8,128)} %get-tuple-element.47.b0_ref.refs_1_), channel_id=1, source_target_pairs={{4,0},{8,4},{12,8},{16,12},{20,16},{24,20},{28,24},{32,28},{36,32}... | collective-permute-start | bytes 6291464 | tf_op jit(solution)/shard_map/ppermute | solution.py:205
  100.2 5.0 %collective-permute-start.5 = (f32[2,136,128]{2,1,0:T(8,128)S(1)}, f32[2,136,128]{2,1,0:T(8,128)S(1)}, u32[]{:S(2)}, u32[]{:S(2)}) collective-permute-start(f32[2,136,128]{2,1,0:T(8,128)S(1)} %get-tuple-element.53.g0_ref), channel_id=1, source_target_pairs={{0,1},{1,0},{2,3},{3,2},{4,5},{5,4},{6,7},{7,6},{8,9},{9,8},{10,11... | collective-permute-start | bytes 417800 | tf_op jit(solution)/shard_map/ppermute | solution.py:210
  102.0 49.4 %collective-permute-start.6 = (f32[2,136,128]{2,1,0:T(8,128)S(1)}, f32[2,136,128]{2,1,0:T(8,128)S(1)}, u32[]{:S(2)}, u32[]{:S(2)}) collective-permute-start(f32[2,136,128]{2,1,0:T(8,128)S(1)} %get-tuple-element.53.g0_ref), channel_id=1, source_target_pairs={{0,2},{1,3},{2,0},{3,1},{4,6},{5,7},{6,4},{7,5},{8,10},{9,11},{10,... | collective-permute-start | bytes 417800 | tf_op jit(solution)/shard_map/ppermute | solution.py:210
  104.7 49.7 %collective-permute-start.7 = (f32[2,136,128]{2,1,0:T(8,128)S(1)}, f32[2,136,128]{2,1,0:T(8,128)S(1)}, u32[]{:S(2)}, u32[]{:S(2)}) collective-permute-start(f32[2,136,128]{2,1,0:T(8,128)S(1)} %get-tuple-element.53.g0_ref), channel_id=1, source_target_pairs={{0,3},{1,2},{2,1},{3,0},{4,7},{5,6},{6,5},{7,4},{8,11},{9,10},{10,... | collective-permute-start | bytes 417800 | tf_op jit(solution)/shard_map/ppermute | solution.py:210
  170.2 98.0 %collective-permute-start.15 = (f32[4096,128]{1,0:T(8,128)S(1)}, f32[4096,128]{1,0:T(8,128)S(1)}, u32[]{:S(2)}, u32[]{:S(2)}) collective-permute-start(f32[4096,128]{1,0:T(8,128)S(1)} %get-tuple-element.60.t1_ref.refs_2_), channel_id=1, source_target_pairs={{0,4},{4,8},{8,12},{12,16},{16,20},{20,24},{24,28},{28,32},{32,36}... | collective-permute-start | bytes 6291464 | tf_op jit(solution)/shard_map/ppermute | solution.py:205
  171.5 96.8 %collective-permute-start.16 = (f32[4096,128]{1,0:T(8,128)S(1)}, f32[4096,128]{1,0:T(8,128)}, u32[]{:S(2)}, u32[]{:S(2)}) collective-permute-start(f32[4096,128]{1,0:T(8,128)S(1)} %get-tuple-element.59.b0_ref.refs_1_), channel_id=1, source_target_pairs={{4,0},{8,4},{12,8},{16,12},{20,16},{24,20},{28,24},{32,28},{36,32}... | collective-permute-start | bytes 6291464 | tf_op jit(solution)/shard_map/ppermute | solution.py:205
  176.9 44.8 %collective-permute-start.10 = (f32[256,128]{1,0:T(8,128)S(1)}, f32[256,128]{1,0:T(8,128)S(1)}, u32[]{:S(2)}, u32[]{:S(2)}) collective-permute-start(f32[256,128]{1,0:T(8,128)S(1)} %get-tuple-element.63), channel_id=1, source_target_pairs={{0,4},{4,8},{8,12},{12,16},{16,20},{20,24},{24,28},{28,32},{32,36}... | collective-permute-start | bytes 393224 | tf_op jit(solution)/shard_map/ppermute | solution.py:205
  178.2 44.4 %collective-permute-start.11 = (f32[256,128]{1,0:T(8,128)S(1)}, f32[256,128]{1,0:T(8,128)S(1)}, u32[]{:S(2)}, u32[]{:S(2)}) collective-permute-start(f32[256,128]{1,0:T(8,128)S(1)} %get-tuple-element.64), channel_id=1, source_target_pairs={{4,0},{8,4},{12,8},{16,12},{20,16},{24,20},{28,24},{32,28},{36,32}... | collective-permute-start | bytes 393224 | tf_op jit(solution)/shard_map/ppermute | solution.py:205
  233.3 4.7 %collective-permute-start.12 = (f32[2,136,128]{2,1,0:T(8,128)S(1)}, f32[2,136,128]{2,1,0:T(8,128)S(1)}, u32[]{:S(2)}, u32[]{:S(2)}) collective-permute-start(f32[2,136,128]{2,1,0:T(8,128)S(1)} %get-tuple-element.67.g0_ref), channel_id=1, source_target_pairs={{0,1},{1,0},{2,3},{3,2},{4,5},{5,4},{6,7},{7,6},{8,9},{9,8},{10,11... | collective-permute-start | bytes 417800 | tf_op jit(solution)/shard_map/ppermute | solution.py:210
  234.9 6.8 %collective-permute-start.13 = (f32[2,136,128]{2,1,0:T(8,128)S(1)}, f32[2,136,128]{2,1,0:T(8,128)S(1)}, u32[]{:S(2)}, u32[]{:S(2)}) collective-permute-start(f32[2,136,128]{2,1,0:T(8,128)S(1)} %get-tuple-element.67.g0_ref), channel_id=1, source_target_pairs={{0,2},{1,3},{2,0},{3,1},{4,6},{5,7},{6,4},{7,5},{8,10},{9,11},{10,... | collective-permute-start | bytes 417800 | tf_op jit(solution)/shard_map/ppermute | solution.py:210
  235.0 12.6 %collective-permute-start.14 = (f32[2,136,128]{2,1,0:T(8,128)S(1)}, f32[2,136,128]{2,1,0:T(8,128)S(1)}, u32[]{:S(2)}, u32[]{:S(2)}) collective-permute-start(f32[2,136,128]{2,1,0:T(8,128)S(1)} %get-tuple-element.67.g0_ref), channel_id=1, source_target_pairs={{0,3},{1,2},{2,1},{3,0},{4,7},{5,6},{6,5},{7,4},{8,11},{9,10},{10,... | collective-permute-start | bytes 417800 | tf_op jit(solution)/shard_map/ppermute | solution.py:210
  255.6 12.7 %collective-permute-start.17 = (f32[256,128]{1,0:T(8,128)S(1)}, f32[256,128]{1,0:T(8,128)S(1)}, u32[]{:S(2)}, u32[]{:S(2)}) collective-permute-start(f32[256,128]{1,0:T(8,128)S(1)} %get-tuple-element.73), channel_id=1, source_target_pairs={{0,4},{4,8},{8,12},{12,16},{16,20},{20,24},{24,28},{28,32},{32,36}... | collective-permute-start | bytes 393224 | tf_op jit(solution)/shard_map/ppermute | solution.py:205
  256.9 11.4 %collective-permute-start.18 = (f32[256,128]{1,0:T(8,128)S(1)}, f32[256,128]{1,0:T(8,128)S(1)}, u32[]{:S(2)}, u32[]{:S(2)}) collective-permute-start(f32[256,128]{1,0:T(8,128)S(1)} %get-tuple-element.74), channel_id=1, source_target_pairs={{4,0},{8,4},{12,8},{16,12},{20,16},{24,20},{28,24},{32,28},{36,32}... | collective-permute-start | bytes 393224 | tf_op jit(solution)/shard_map/ppermute | solution.py:205
  279.0 3.7 %collective-permute-start.19 = (f32[2,136,128]{2,1,0:T(8,128)S(1)}, f32[2,136,128]{2,1,0:T(8,128)S(1)}, u32[]{:S(2)}, u32[]{:S(2)}) collective-permute-start(f32[2,136,128]{2,1,0:T(8,128)S(1)} %get-tuple-element.77.g0_ref), channel_id=1, source_target_pairs={{0,1},{1,0},{2,3},{3,2},{4,5},{5,4},{6,7},{7,6},{8,9},{9,8},{10,11... | collective-permute-start | bytes 417800 | tf_op jit(solution)/shard_map/ppermute | solution.py:210
  279.0 6.4 %collective-permute-start.20 = (f32[2,136,128]{2,1,0:T(8,128)S(1)}, f32[2,136,128]{2,1,0:T(8,128)S(1)}, u32[]{:S(2)}, u32[]{:S(2)}) collective-permute-start(f32[2,136,128]{2,1,0:T(8,128)S(1)} %get-tuple-element.77.g0_ref), channel_id=1, source_target_pairs={{0,2},{1,3},{2,0},{3,1},{4,6},{5,7},{6,4},{7,5},{8,10},{9,11},{10,... | collective-permute-start | bytes 417800 | tf_op jit(solution)/shard_map/ppermute | solution.py:210
  279.1 9.9 %collective-permute-start.21 = (f32[2,136,128]{2,1,0:T(8,128)S(1)}, f32[2,136,128]{2,1,0:T(8,128)S(1)}, u32[]{:S(2)}, u32[]{:S(2)}) collective-permute-start(f32[2,136,128]{2,1,0:T(8,128)S(1)} %get-tuple-element.77.g0_ref), channel_id=1, source_target_pairs={{0,3},{1,2},{2,1},{3,0},{4,7},{5,6},{6,5},{7,4},{8,11},{9,10},{10,... | collective-permute-start | bytes 417800 | tf_op jit(solution)/shard_map/ppermute | solution.py:210
  (11 other events, 310.9 us)

commit v2 on v1

--- a/solution.py
+++ b/solution.py
@@ -11,9 +11,9 @@
 ITERS = 12
 EPS = 1e-06
 DAMPING = 0.04
-CHUNKS = 1
 TILE = 512
 GROWS = 136
+RELAY = 5
 F32 = jnp.float32
 BF16 = jnp.bfloat16
 PARAMS = pltpu.CompilerParams(vmem_limit_bytes=40 * 1024 * 1024)
@@ -110,8 +110,11 @@
     )(flags, *blocks, *rebuilt, g_in)
 
 
-def polar_kernel(g0_ref, g1_ref, g2_ref, g3_ref, q_ref, right_ref, left_ref):
-    total = (g0_ref[...] + g1_ref[...]) + (g2_ref[...] + g3_ref[...])
+def polar_kernel(*refs):
+    *g_refs, q_ref, right_ref, left_ref = refs
+    total = g_refs[0][...]
+    for g_ref in g_refs[1:]:
+        total = total + g_ref[...]
     eye = (lax.broadcasted_iota(jnp.int32, (B, B), 0) == lax.broadcasted_iota(jnp.int32, (B, B), 1)).astype(F32)
     chains = []
     for pair in range(2):
@@ -205,9 +208,18 @@
     return lax.ppermute(value, "pair", [(source, source + steps) for source in range(initial, last)])
 
 
-def row_terms(value):
-    count = lax.axis_size("row")
-    return [value] + [lax.ppermute(value, "row", [(i, i ^ k) for i in range(count)]) for k in range(1, count)]
+def row_terms(g, relayed):
+    rows, pairs = lax.axis_size("row"), lax.axis_size("pair")
+    part = g + lax.ppermute(g, "row", [(r, r ^ 1) for r in range(rows)])
+    if not relayed:
+        return [part, lax.ppermute(part, "row", [(r, r ^ 2) for r in range(rows)])]
+    both = ("pair", "row")
+    relay = {0: RELAY, pairs - 1: pairs - 1 - RELAY}
+    here = [p * rows + r for p in range(pairs) if p not in relay for r in range(rows)]
+    ends = [(p * rows + r, via * rows + r) for p, via in relay.items() for r in range(rows)]
+    hop = lax.ppermute(part, both, [(end, via ^ 2) for end, via in ends])
+    direct = lax.ppermute(part, both, [(i, i ^ 2) for i in here])
+    return [part, direct, lax.ppermute(hop, both, [(via, end) for end, via in ends])]
 
 
 def after(values, done):
@@ -219,7 +231,7 @@
     flags = jnp.stack([position == 0, position == lax.axis_size("pair") - 1]).astype(jnp.int32)
     zero = jnp.zeros((2, GROWS, B), F32)
 
-    q, _, _ = polar(row_terms(gram_first(factor)))
+    q, _, _ = polar(row_terms(gram_first(factor), False))
     right, left, t1, b0 = rotate(flags, [factor], q)
     arrived = (shifted(right, 1), shifted(left, -1))
     (t1, b0), arrived = after((t1, b0), arrived)
@@ -228,7 +240,7 @@
     rebuilt = ()
     for step in range(1, STEPS):
         g, t0, b1 = gram_next(flags, (left, right, b0, t1, *arrived), rebuilt, zero)
-        q, q_right, q_left = polar(row_terms(g))
+        q, q_right, q_left = polar(row_terms(g, step < STEPS - 1))
         if step == STEPS - 1:
             return rotate(flags, [t0, b0, t1, b1], q, last=True)
         q_top, q_bottom = shifted(q_right, 1), shifted(q_left, -1)
@@ -238,7 +250,7 @@
         rebuilt = (*older, q_top, q_bottom)
         arrived = ahead
         if step < STEPS - 2:
-            (t1, b0), arrived = after((t1, b0), arrived)
+            (t1, b0), (arrived, rebuilt) = after((t1, b0), (arrived, rebuilt))
             ahead = (shifted(t1, 1), shifted(b0, -1))
 
 

time: 306 us -> 240 us (0.78)
  the two profiles are of different devices: /device:TPU:63 before, /device:TPU:30 now
where the time goes in v2:
time: 240 us; the launch traced here: 239 us
  Pallas kernels  94.8 us (40%)
  waiting for transfers between devices  81.3 us (34%)
  starting transfers between devices  54.4 us (23%)
  local copies, waits for them, and re-layouts  7.45 us (3%)
    ppermute x10, waiting for transfers between devices, shifted(): lax.ppermute(value, 'pair', [(source, source + steps) for source in range...  61.5 us
    pallas_call x4, Pallas kernels, polar(): pl.pallas_call(polar_kernel, out_shape=[jax.ShapeDtypeStruct((2, 2 * B, 2...  33.2 us
    ppermute x10, starting transfers between devices, shifted(): lax.ppermute(value, 'pair', [(source, source + steps) for source in range...  32.9 us
    pallas_call x4, Pallas kernels, rotate(): pl.pallas_call(functools.partial(rotate_kernel, whole, last), grid=(rows...  32.2 us
    pallas_call x3, Pallas kernels, gram_next(): pl.pallas_call(functools.partial(gram_next_kernel, bool(rebuilt)), grid=(...  26 us
    ppermute x2, starting transfers between devices, row_terms(): direct = lax.ppermute(part, both, [(i, i ^ 2) for i in here])  11 us
    ppermute x2, waiting for transfers between devices, row_terms(): return [part, lax.ppermute(part, 'row', [(r, r ^ 2) for r in range(rows)])]  7.89 us
    ppermute x2, starting transfers between devices, row_terms(): return [part, lax.ppermute(part, 'row', [(r, r ^ 2) for r in range(rows)])]  7.61 us
  transfers between devices with their start and end apart: 22, of which 13 were waited for; matrix products, arithmetic and copies ran while one was open for 0% of the time, Pallas kernels for 20%

profile of v2, /device:TPU:30, one launch (start us, length us, event | category | flops | bytes accessed | tf_op | source)
XLA Modules:
  0.0 238.5 jit_solution(13898322439354938779)
XLA Ops:
  8.2 4.0 %collective-permute-start.1 = (f32[2,136,128]{2,1,0:T(8,128)S(1)}, f32[2,136,128]{2,1,0:T(8,128)S(1)}, u32[]{:S(2)}, u32[]{:S(2)}) collective-permute-start(f32[2,136,128]{2,1,0:T(8,128)S(1)} %add.12.refs_0_), channel_id=1, source_target_pairs={{0,2},{1,3},{2,0},{3,1},{4,6},{5,7},{6,4},{7,5},{8,10},{9,11},{10,... | collective-permute-start | bytes 417800 | tf_op jit(solution)/shard_map/ppermute | solution.py:215
  12.2 3.9 %collective-permute-done.1.refs_1_ = f32[2,136,128]{2,1,0:T(8,128)S(1)} collective-permute-done((f32[2,136,128]{2,1,0:T(8,128)S(1)}, f32[2,136,128]{2,1,0:T(8,128)S(1)}, u32[]{:S(2)}, u32[]{:S(2)}) %collective-permute-start.1) | collective-permute-done | bytes 139296 | tf_op jit(solution)/shard_map/ppermute | solution.py:215
  16.2 8.6 %polar.4 = (f32[2,256,256]{2,1,0:T(8,128)S(1)}, f32[256,128]{1,0:T(8,128)}, f32[256,128]{1,0:T(8,128)}) custom-call(f32[2,136,128]{2,1,0:T(8,128)S(1)} %add.12.refs_0_, f32[2,136,128]{2,1,0:T(8,128)S(1)} %collective-permute-done.1.refs_1_), custom_call_target="tpu_custom_call" | custom-call | tf_op jit(solution)/shard_map/polar/pallas_call | solution.py:149
  24.8 9.6 %rotate.4 = (f32[4096,128]{1,0:T(8,128)S(1)}, f32[4096,128]{1,0:T(8,128)S(1)}, f32[4096,128]{1,0:T(8,128)}, f32[4096,128]{1,0:T(8,128)}) custom-call(s32[2]{0:T(128)S(1)} %add_convert_fusion.flag_ref, f32[4096,512]{1,0:T(8,128)} %refs_0_.1, f32[2,256,256]{2,1,0:T(8,128)S(1)} %get-tuple-element.46.refs_1_), custom_call_target="tpu_custom_call" | custom-call | tf_op jit(solution)/shard_map/rotate/pallas_call | solution.py:194
  40.2 43.2 %collective-permute-done.2.in_top_ref = f32[4096,128]{1,0:T(8,128)S(1)} collective-permute-done((f32[4096,128]{1,0:T(8,128)S(1)}, f32[4096,128]{1,0:T(8,128)S(1)}, u32[]{:S(2)}, u32[]{:S(2)}) %collective-permute-start.2) | collective-permute-done | bytes 2097184 | tf_op jit(solution)/shard_map/ppermute | solution.py:208
  83.4 6.4 %collective-permute-done.3.in_bottom_ref = f32[4096,128]{1,0:T(8,128)S(1)} collective-permute-done((f32[4096,128]{1,0:T(8,128)S(1)}, f32[4096,128]{1,0:T(8,128)S(1)}, u32[]{:S(2)}, u32[]{:S(2)}) %collective-permute-start.3) | collective-permute-done | bytes 2097184 | tf_op jit(solution)/shard_map/ppermute | solution.py:208
  91.7 3.9 %collective-permute-start.9 = (f32[4096,128]{1,0:T(8,128)}, f32[4096,128]{1,0:T(8,128)S(1)}, u32[]{:S(2)}, u32[]{:S(2)}) collective-permute-start(f32[4096,128]{1,0:T(8,128)} %get-tuple-element.51.b0_ref.refs_1_), channel_id=1, source_target_pairs={{4,0},{8,4},{12,8},{16,12},{20,16},{24,20},{28,24},{32,28},{36,32}... | collective-permute-start | bytes 6291464 | tf_op jit(solution)/shard_map/ppermute | solution.py:208
  95.7 7.4 %gram_next.3 = (f32[2,136,128]{2,1,0:T(8,128)S(1)}, f32[4096,128]{1,0:T(8,128)S(1)}, f32[4096,128]{1,0:T(8,128)S(1)}) custom-call(s32[2]{0:T(128)S(1)} %add_convert_fusion.flag_ref, f32[4096,128]{1,0:T(8,128)S(1)} %get-tuple-element.69.first_ref.rest_0_, f32[4096,128]{1,0:T(8,128)S(1)} %get-tuple-element.70.last_ref.rest_1_, ...), custom_call_target="tpu_custom_call" | custom-call | tf_op jit(solution)/shard_map/gram_next/pallas_call | solution.py:102
  106.5 5.5 %collective-permute-start.5 = (f32[2,136,128]{2,1,0:T(8,128)S(1)}, f32[2,136,128]{2,1,0:T(8,128)S(1)}, u32[]{:S(2)}, u32[]{:S(2)}) collective-permute-start(f32[2,136,128]{2,1,0:T(8,128)S(1)} %add.13.refs_0_), channel_id=1, source_target_pairs={{4,6},{5,7},{6,4},{7,5},{8,10},{9,11},{10,8},{11,9},{12,14},{13,15... | collective-permute-start | bytes 417800 | tf_op jit(solution)/shard_map/ppermute | solution.py:221
  116.0 8.0 %polar.5 = (f32[2,256,256]{2,1,0:T(8,128)S(1)}, f32[256,128]{1,0:T(8,128)S(1)}, f32[256,128]{1,0:T(8,128)S(1)}) custom-call(f32[2,136,128]{2,1,0:T(8,128)S(1)} %add.13.refs_0_, f32[2,136,128]{2,1,0:T(8,128)S(1)} %collective-permute-done.5.refs_1_, f32[2,136,128]{2,1,0:T(8,128)S(1)} %collective-permute-done.7.refs_2_), custom_call_target="tpu_custom_call" | custom-call | tf_op jit(solution)/shard_map/polar/pallas_call | solution.py:149
  124.0 5.8 %collective-permute-start.10 = (f32[256,128]{1,0:T(8,128)S(1)}, f32[256,128]{1,0:T(8,128)S(1)}, u32[]{:S(2)}, u32[]{:S(2)}) collective-permute-start(f32[256,128]{1,0:T(8,128)S(1)} %get-tuple-element.63), channel_id=1, source_target_pairs={{0,4},{4,8},{8,12},{12,16},{16,20},{20,24},{24,28},{28,32},{32,36}... | collective-permute-start | bytes 393224 | tf_op jit(solution)/shard_map/ppermute | solution.py:208
  131.7 7.8 %rotate.5 = (f32[4096,128]{1,0:T(8,128)S(1)}, f32[4096,128]{1,0:T(8,128)S(1)}, f32[4096,128]{1,0:T(8,128)S(1)}, f32[4096,128]{1,0:T(8,128)S(1)}) custom-call(s32[2]{0:T(128)S(1)} %add_convert_fusion.flag_ref, f32[4096,128]{1,0:T(8,128)S(1)} %get-tuple-element.55.refs_0_, f32[4096,128]{1,0:T(8,128)} %get-tuple-element.51.b0_ref.refs_1_, ...), custom_call_target="tpu_custom_call" | custom-call | tf_op jit(solution)/shard_map/rotate/pallas_call | solution.py:194
  140.4 6.1 %collective-permute-done.11.rest_3_ = f32[256,128]{1,0:T(8,128)S(1)} collective-permute-done((f32[256,128]{1,0:T(8,128)S(1)}, f32[256,128]{1,0:T(8,128)S(1)}, u32[]{:S(2)}, u32[]{:S(2)}) %collective-permute-start.11) | collective-permute-done | bytes 131104 | tf_op jit(solution)/shard_map/ppermute | solution.py:208
  148.5 3.9 %collective-permute-start.17 = (f32[4096,128]{1,0:T(8,128)S(1)}, f32[4096,128]{1,0:T(8,128)}, u32[]{:S(2)}, u32[]{:S(2)}) collective-permute-start(f32[4096,128]{1,0:T(8,128)S(1)} %get-tuple-element.65.b0_ref.refs_1_), channel_id=1, source_target_pairs={{4,0},{8,4},{12,8},{16,12},{20,16},{24,20},{28,24},{32,28},{36,32}... | collective-permute-start | bytes 6291464 | tf_op jit(solution)/shard_map/ppermute | solution.py:208
  152.4 9.3 %gram_next.4 = (f32[2,136,128]{2,1,0:T(8,128)S(1)}, f32[4096,128]{1,0:T(8,128)S(1)}, f32[4096,128]{1,0:T(8,128)S(1)}) custom-call(s32[2]{0:T(128)S(1)} %add_convert_fusion.flag_ref, f32[4096,128]{1,0:T(8,128)S(1)} %get-tuple-element.59.first_ref.rest_0_, f32[4096,128]{1,0:T(8,128)S(1)} %get-tuple-element.60.last_ref.rest_1_, ...), custom_call_target="tpu_custom_call" | custom-call | tf_op jit(solution)/shard_map/gram_next/pallas_call | solution.py:102
  165.2 5.5 %collective-permute-start.13 = (f32[2,136,128]{2,1,0:T(8,128)S(1)}, f32[2,136,128]{2,1,0:T(8,128)S(1)}, u32[]{:S(2)}, u32[]{:S(2)}) collective-permute-start(f32[2,136,128]{2,1,0:T(8,128)S(1)} %add.14.refs_0_), channel_id=1, source_target_pairs={{4,6},{5,7},{6,4},{7,5},{8,10},{9,11},{10,8},{11,9},{12,14},{13,15... | collective-permute-start | bytes 417800 | tf_op jit(solution)/shard_map/ppermute | solution.py:221
  174.6 8.0 %polar.6 = (f32[2,256,256]{2,1,0:T(8,128)S(1)}, f32[256,128]{1,0:T(8,128)S(1)}, f32[256,128]{1,0:T(8,128)S(1)}) custom-call(f32[2,136,128]{2,1,0:T(8,128)S(1)} %add.14.refs_0_, f32[2,136,128]{2,1,0:T(8,128)S(1)} %collective-permute-done.13.refs_1_, f32[2,136,128]{2,1,0:T(8,128)S(1)} %collective-permute-done.15.refs_2_), custom_call_target="tpu_custom_call" | custom-call | tf_op jit(solution)/shard_map/polar/pallas_call | solution.py:149
  182.6 5.8 %collective-permute-start.18 = (f32[256,128]{1,0:T(8,128)S(1)}, f32[256,128]{1,0:T(8,128)S(1)}, u32[]{:S(2)}, u32[]{:S(2)}) collective-permute-start(f32[256,128]{1,0:T(8,128)S(1)} %get-tuple-element.81), channel_id=1, source_target_pairs={{0,4},{4,8},{8,12},{12,16},{16,20},{20,24},{24,28},{28,32},{32,36}... | collective-permute-start | bytes 393224 | tf_op jit(solution)/shard_map/ppermute | solution.py:208
  190.3 7.4 %rotate.6 = (f32[4096,128]{1,0:T(8,128)S(1)}, f32[4096,128]{1,0:T(8,128)S(1)}, f32[4096,128]{1,0:T(8,128)S(1)}, f32[4096,128]{1,0:T(8,128)S(1)}) custom-call(s32[2]{0:T(128)S(1)} %add_convert_fusion.flag_ref, f32[4096,128]{1,0:T(8,128)S(1)} %get-tuple-element.73.refs_0_, f32[4096,128]{1,0:T(8,128)S(1)} %get-tuple-element.65.b0_ref.refs_1_, ...), custom_call_target="tpu_custom_call" | custom-call | tf_op jit(solution)/shard_map/rotate/pallas_call | solution.py:194
  197.8 4.9 %collective-permute-done.19.rest_3_ = f32[256,128]{1,0:T(8,128)S(1)} collective-permute-done((f32[256,128]{1,0:T(8,128)S(1)}, f32[256,128]{1,0:T(8,128)S(1)}, u32[]{:S(2)}, u32[]{:S(2)}) %collective-permute-start.19) | collective-permute-done | bytes 131104 | tf_op jit(solution)/shard_map/ppermute | solution.py:208
  204.0 9.3 %gram_next.5 = (f32[2,136,128]{2,1,0:T(8,128)S(1)}, f32[4096,128]{1,0:T(8,128)S(1)}, f32[4096,128]{1,0:T(8,128)S(1)}) custom-call(s32[2]{0:T(128)S(1)} %add_convert_fusion.flag_ref, f32[4096,128]{1,0:T(8,128)S(1)} %get-tuple-element.77.first_ref, f32[4096,128]{1,0:T(8,128)S(1)} %get-tuple-element.78.last_ref, ...), custom_call_target="tpu_custom_call" | custom-call | tf_op jit(solution)/shard_map/gram_next/pallas_call | solution.py:102
  218.4 4.0 %collective-permute-done.21.refs_1_ = f32[2,136,128]{2,1,0:T(8,128)S(1)} collective-permute-done((f32[2,136,128]{2,1,0:T(8,128)S(1)}, f32[2,136,128]{2,1,0:T(8,128)S(1)}, u32[]{:S(2)}, u32[]{:S(2)}) %collective-permute-start.21) | collective-permute-done | bytes 139296 | tf_op jit(solution)/shard_map/ppermute | solution.py:215
  222.4 8.6 %polar.7 = (f32[2,256,256]{2,1,0:T(8,128)S(1)}, f32[256,128]{1,0:T(8,128)}, f32[256,128]{1,0:T(8,128)}) custom-call(f32[2,136,128]{2,1,0:T(8,128)S(1)} %add.15.refs_0_, f32[2,136,128]{2,1,0:T(8,128)S(1)} %collective-permute-done.21.refs_1_), custom_call_target="tpu_custom_call" | custom-call | tf_op jit(solution)/shard_map/polar/pallas_call | solution.py:149
  231.1 7.5 %rotate.7 = f32[4096,512]{1,0:T(8,128)} custom-call(s32[2]{0:T(128)S(1)} %add_convert_fusion.flag_ref, f32[4096,128]{1,0:T(8,128)S(1)} %get-tuple-element.83.refs_0_, f32[4096,128]{1,0:T(8,128)S(1)} %get-tuple-element.79.b0_ref.refs_1_, f32[4096,128]{1,0:T(8,128)S(1)} %get-tuple-element.80.t1_ref.refs_2_, f32[4096,128]{1,0:T(8,128)S(1)} %get-tuple-element.84.refs_3_, ...), custom_call_target="tpu_custom_call" | custom-call | tf_op jit(solution)/shard_map/rotate/pallas_call | solution.py:194
  (64 shorter events, 43.8 us)
Async XLA Ops:
  6.8 1.4 collective-permute-start
  8.2 7.9 %collective-permute-start.1 = (f32[2,136,128]{2,1,0:T(8,128)S(1)}, f32[2,136,128]{2,1,0:T(8,128)S(1)}, u32[]{:S(2)}, u32[]{:S(2)}) collective-permute-start(f32[2,136,128]{2,1,0:T(8,128)S(1)} %add.12.refs_0_), channel_id=1, source_target_pairs={{0,2},{1,3},{2,0},{3,1},{4,6},{5,7},{6,4},{7,5},{8,10},{9,11},{10,... | collective-permute-start | bytes 417800 | tf_op jit(solution)/shard_map/ppermute | solution.py:215
  34.4 68.7 %copy-start.4 = (f32[4096,128]{1,0:T(8,128)}, f32[4096,128]{1,0:T(8,128)S(1)}, u32[]{:S(2)}) copy-start(f32[4096,128]{1,0:T(8,128)S(1)} %get-tuple-element.70.last_ref.rest_1_) | copy-start | bytes 6291460
  34.4 68.7 %copy-start.5 = (f32[4096,128]{1,0:T(8,128)}, f32[4096,128]{1,0:T(8,128)S(1)}, u32[]{:S(2)}) copy-start(f32[4096,128]{1,0:T(8,128)S(1)} %get-tuple-element.69.first_ref.rest_0_) | copy-start | bytes 6291460
  34.4 49.1 %collective-permute-start.2 = (f32[4096,128]{1,0:T(8,128)S(1)}, f32[4096,128]{1,0:T(8,128)S(1)}, u32[]{:S(2)}, u32[]{:S(2)}) collective-permute-start(f32[4096,128]{1,0:T(8,128)S(1)} %get-tuple-element.70.last_ref.rest_1_), channel_id=1, source_target_pairs={{0,4},{4,8},{8,12},{12,16},{16,20},{20,24},{24,28},{28,32},{32,36}... | collective-permute-start | bytes 6291464 | tf_op jit(solution)/shard_map/ppermute | solution.py:208
  37.1 52.7 %collective-permute-start.3 = (f32[4096,128]{1,0:T(8,128)S(1)}, f32[4096,128]{1,0:T(8,128)S(1)}, u32[]{:S(2)}, u32[]{:S(2)}) collective-permute-start(f32[4096,128]{1,0:T(8,128)S(1)} %get-tuple-element.69.first_ref.rest_0_), channel_id=1, source_target_pairs={{4,0},{8,4},{12,8},{16,12},{20,16},{24,20},{28,24},{32,28},{36,32}... | collective-permute-start | bytes 6291464 | tf_op jit(solution)/shard_map/ppermute | solution.py:208
  89.8 56.7 %collective-permute-start.8 = (f32[4096,128]{1,0:T(8,128)}, f32[4096,128]{1,0:T(8,128)S(1)}, u32[]{:S(2)}, u32[]{:S(2)}) collective-permute-start(f32[4096,128]{1,0:T(8,128)} %get-tuple-element.52.t1_ref.refs_2_), channel_id=1, source_target_pairs={{0,4},{4,8},{8,12},{12,16},{16,20},{20,24},{24,28},{28,32},{32,36}... | collective-permute-start | bytes 6291464 | tf_op jit(solution)/shard_map/ppermute | solution.py:208
  91.7 54.8 %collective-permute-start.9 = (f32[4096,128]{1,0:T(8,128)}, f32[4096,128]{1,0:T(8,128)S(1)}, u32[]{:S(2)}, u32[]{:S(2)}) collective-permute-start(f32[4096,128]{1,0:T(8,128)} %get-tuple-element.51.b0_ref.refs_1_), channel_id=1, source_target_pairs={{4,0},{8,4},{12,8},{16,12},{20,16},{24,20},{28,24},{32,28},{36,32}... | collective-permute-start | bytes 6291464 | tf_op jit(solution)/shard_map/ppermute | solution.py:208
  104.5 1.4 collective-permute-start.4
  105.9 6.2 %collective-permute-start.6 = (f32[2,136,128]{2,1,0:T(8,128)S(1)}, f32[2,136,128]{2,1,0:T(8,128)S(1)}, u32[]{:S(2)}, u32[]{:S(2)}) collective-permute-start(f32[2,136,128]{2,1,0:T(8,128)S(1)} %add.13.refs_0_), channel_id=1, source_target_pairs={{0,22},{1,23},{2,20},{3,21},{124,106},{125,107},{126,104},{127,105}} | collective-permute-start | bytes 417800 | tf_op jit(solution)/shard_map/ppermute | solution.py:220
  106.5 9.5 %collective-permute-start.5 = (f32[2,136,128]{2,1,0:T(8,128)S(1)}, f32[2,136,128]{2,1,0:T(8,128)S(1)}, u32[]{:S(2)}, u32[]{:S(2)}) collective-permute-start(f32[2,136,128]{2,1,0:T(8,128)S(1)} %add.13.refs_0_), channel_id=1, source_target_pairs={{4,6},{5,7},{6,4},{7,5},{8,10},{9,11},{10,8},{11,9},{12,14},{13,15... | collective-permute-start | bytes 417800 | tf_op jit(solution)/shard_map/ppermute | solution.py:221
  112.0 4.0 %collective-permute-start.7 = (f32[2,136,128]{2,1,0:T(8,128)S(1)}, f32[2,136,128]{2,1,0:T(8,128)S(1)}, u32[]{:S(2)}, u32[]{:S(2)}) collective-permute-start(f32[2,136,128]{2,1,0:T(8,128)S(1)} %collective-permute-done.6), channel_id=1, source_target_pairs={{20,0},{21,1},{22,2},{23,3},{104,124},{105,125},{106,126},{107,127}} | collective-permute-start | bytes 417800 | tf_op jit(solution)/shard_map/ppermute | solution.py:222
  124.0 16.4 %collective-permute-start.10 = (f32[256,128]{1,0:T(8,128)S(1)}, f32[256,128]{1,0:T(8,128)S(1)}, u32[]{:S(2)}, u32[]{:S(2)}) collective-permute-start(f32[256,128]{1,0:T(8,128)S(1)} %get-tuple-element.63), channel_id=1, source_target_pairs={{0,4},{4,8},{8,12},{12,16},{16,20},{20,24},{24,28},{28,32},{32,36}... | collective-permute-start | bytes 393224 | tf_op jit(solution)/shard_map/ppermute | solution.py:208
  129.8 16.7 %collective-permute-start.11 = (f32[256,128]{1,0:T(8,128)S(1)}, f32[256,128]{1,0:T(8,128)S(1)}, u32[]{:S(2)}, u32[]{:S(2)}) collective-permute-start(f32[256,128]{1,0:T(8,128)S(1)} %get-tuple-element.64), channel_id=1, source_target_pairs={{4,0},{8,4},{12,8},{16,12},{20,16},{24,20},{28,24},{32,28},{36,32}... | collective-permute-start | bytes 393224 | tf_op jit(solution)/shard_map/ppermute | solution.py:208
  146.5 56.2 %collective-permute-start.16 = (f32[4096,128]{1,0:T(8,128)S(1)}, f32[4096,128]{1,0:T(8,128)S(1)}, u32[]{:S(2)}, u32[]{:S(2)}) collective-permute-start(f32[4096,128]{1,0:T(8,128)S(1)} %get-tuple-element.66.t1_ref.refs_2_), channel_id=1, source_target_pairs={{0,4},{4,8},{8,12},{12,16},{16,20},{20,24},{24,28},{28,32},{32,36}... | collective-permute-start | bytes 6291464 | tf_op jit(solution)/shard_map/ppermute | solution.py:208
  148.5 54.2 %collective-permute-start.17 = (f32[4096,128]{1,0:T(8,128)S(1)}, f32[4096,128]{1,0:T(8,128)}, u32[]{:S(2)}, u32[]{:S(2)}) collective-permute-start(f32[4096,128]{1,0:T(8,128)S(1)} %get-tuple-element.65.b0_ref.refs_1_), channel_id=1, source_target_pairs={{4,0},{8,4},{12,8},{16,12},{20,16},{24,20},{28,24},{32,28},{36,32}... | collective-permute-start | bytes 6291464 | tf_op jit(solution)/shard_map/ppermute | solution.py:208
  163.1 1.4 collective-permute-start.12
  164.5 6.2 %collective-permute-start.14 = (f32[2,136,128]{2,1,0:T(8,128)S(1)}, f32[2,136,128]{2,1,0:T(8,128)S(1)}, u32[]{:S(2)}, u32[]{:S(2)}) collective-permute-start(f32[2,136,128]{2,1,0:T(8,128)S(1)} %add.14.refs_0_), channel_id=1, source_target_pairs={{0,22},{1,23},{2,20},{3,21},{124,106},{125,107},{126,104},{127,105}} | collective-permute-start | bytes 417800 | tf_op jit(solution)/shard_map/ppermute | solution.py:220
  165.2 9.5 %collective-permute-start.13 = (f32[2,136,128]{2,1,0:T(8,128)S(1)}, f32[2,136,128]{2,1,0:T(8,128)S(1)}, u32[]{:S(2)}, u32[]{:S(2)}) collective-permute-start(f32[2,136,128]{2,1,0:T(8,128)S(1)} %add.14.refs_0_), channel_id=1, source_target_pairs={{4,6},{5,7},{6,4},{7,5},{8,10},{9,11},{10,8},{11,9},{12,14},{13,15... | collective-permute-start | bytes 417800 | tf_op jit(solution)/shard_map/ppermute | solution.py:221
  170.7 4.0 %collective-permute-start.15 = (f32[2,136,128]{2,1,0:T(8,128)S(1)}, f32[2,136,128]{2,1,0:T(8,128)S(1)}, u32[]{:S(2)}, u32[]{:S(2)}) collective-permute-start(f32[2,136,128]{2,1,0:T(8,128)S(1)} %collective-permute-done.14), channel_id=1, source_target_pairs={{20,0},{21,1},{22,2},{23,3},{104,124},{105,125},{106,126},{107,127}} | collective-permute-start | bytes 417800 | tf_op jit(solution)/shard_map/ppermute | solution.py:222
  182.6 15.2 %collective-permute-start.18 = (f32[256,128]{1,0:T(8,128)S(1)}, f32[256,128]{1,0:T(8,128)S(1)}, u32[]{:S(2)}, u32[]{:S(2)}) collective-permute-start(f32[256,128]{1,0:T(8,128)S(1)} %get-tuple-element.81), channel_id=1, source_target_pairs={{0,4},{4,8},{8,12},{12,16},{16,20},{20,24},{24,28},{28,32},{32,36}... | collective-permute-start | bytes 393224 | tf_op jit(solution)/shard_map/ppermute | solution.py:208
  188.4 14.3 %collective-permute-start.19 = (f32[256,128]{1,0:T(8,128)S(1)}, f32[256,128]{1,0:T(8,128)S(1)}, u32[]{:S(2)}, u32[]{:S(2)}) collective-permute-start(f32[256,128]{1,0:T(8,128)S(1)} %get-tuple-element.82), channel_id=1, source_target_pairs={{4,0},{8,4},{12,8},{16,12},{20,16},{24,20},{28,24},{32,28},{36,32}... | collective-permute-start | bytes 393224 | tf_op jit(solution)/shard_map/ppermute | solution.py:208
  213.3 1.4 collective-permute-start.20
  214.8 7.6 %collective-permute-start.21 = (f32[2,136,128]{2,1,0:T(8,128)S(1)}, f32[2,136,128]{2,1,0:T(8,128)S(1)}, u32[]{:S(2)}, u32[]{:S(2)}) collective-permute-start(f32[2,136,128]{2,1,0:T(8,128)S(1)} %add.15.refs_0_), channel_id=1, source_target_pairs={{0,2},{1,3},{2,0},{3,1},{4,6},{5,7},{6,4},{7,5},{8,10},{9,11},{10,... | collective-permute-start | bytes 417800 | tf_op jit(solution)/shard_map/ppermute | solution.py:215
  (11 other events, 104.1 us)

commit v3 on v2

--- a/solution.py
+++ b/solution.py
@@ -11,12 +11,12 @@
 ITERS = 12
 EPS = 1e-06
 DAMPING = 0.04
-TILE = 512
+TILE = 1024
 GROWS = 136
 RELAY = 5
 F32 = jnp.float32
 BF16 = jnp.bfloat16
-PARAMS = pltpu.CompilerParams(vmem_limit_bytes=40 * 1024 * 1024)
+PARAMS = pltpu.CompilerParams(vmem_limit_bytes=24 * 1024 * 1024)
 NN = (((1,), (0,)), ((), ()))
 NT = (((1,), (1,)), ((), ()))
 TN = (((0,), (0,)), ((), ()))
@@ -37,6 +37,11 @@
 
 def beside(a, b):
     return jnp.concatenate([a, b], axis=1)
+
+
+def dot3_narrow(a, b):
+    y = dot(a[0], beside(*b))
+    return (y[:, :B] + y[:, B:]) + dot(a[1], b[0])
 
 
 def add_gram(g_ref, pair, top, bottom):
@@ -82,8 +87,8 @@
 
     in_top, in_bottom = in_top_ref[...], in_bottom_ref[...]
     if rebuild:
-        in_top = dot3(halves(beside(in_top, prev_left_ref[...])), halves(q_top_ref[...]))
-        in_bottom = dot3(halves(beside(prev_right_ref[...], in_bottom)), halves(q_bottom_ref[...]))
+        in_top = dot3_narrow(halves(beside(in_top, prev_left_ref[...])), halves(q_top_ref[...]))
+        in_bottom = dot3_narrow(halves(beside(prev_right_ref[...], in_bottom)), halves(q_bottom_ref[...]))
     t0 = jnp.where(flag_ref[0] == 1, first_ref[...], in_top)
     b1 = jnp.where(flag_ref[1] == 1, last_ref[...], in_bottom)
     t0_ref[...] = t0
@@ -110,7 +115,7 @@
     )(flags, *blocks, *rebuilt, g_in)
 
 
-def polar_kernel(*refs):
+def polar_kernel(swap, flag_ref, *refs):
     *g_refs, q_ref, right_ref, left_ref = refs
     total = g_refs[0][...]
     for g_ref in g_refs[1:]:
@@ -135,19 +140,23 @@
         inner = [halves(dot3(part, part, NT)) for part in parts]
         return tuple(1.5 * chain - 0.5 * dot3(m, part) for chain, m, part in zip(chains, inner, parts))
 
-    chains = lax.fori_loop(0, ITERS, iterate, tuple(chains))
-    for pair in range(2):
-        q_ref[pair, :B, :] = chains[2 * pair]
-        q_ref[pair, B:, :] = chains[2 * pair + 1]
-    right_ref[:B, :] = chains[2][:, :B]
-    right_ref[B:, :] = chains[3][:, :B]
-    left_ref[:B, :] = chains[0][:, B:]
-    left_ref[B:, :] = chains[1][:, B:]
-
-
-def polar(grams):
-    return pl.pallas_call(
-        polar_kernel,
+    chains = lax.fori_loop(0, ITERS, iterate, tuple(chains), unroll=ITERS)
+    for half in range(2):
+        rows = pl.ds(half * B, B)
+        top, bottom = chains[half][:, :B], chains[half][:, B:]
+        left_ref[rows, :] = bottom
+        if swap:
+            first = flag_ref[0] == 1
+            top, bottom = jnp.where(first, bottom, top), jnp.where(first, top, bottom)
+        q_ref[0, rows, :] = beside(top, bottom)
+        q_ref[1, rows, :] = chains[2 + half]
+        right_ref[rows, :] = chains[2 + half][:, :B]
+
+
+def polar(flags, grams, swap=True):
+    return pl.pallas_call(
+        functools.partial(polar_kernel, swap),
+        in_specs=[pl.BlockSpec(memory_space=pltpu.SMEM)] + [pl.BlockSpec(memory_space=pltpu.VMEM)] * len(grams),
         out_shape=[
             jax.ShapeDtypeStruct((2, 2 * B, 2 * B), F32),
             jax.ShapeDtypeStruct((2 * B, B), F32),
@@ -155,51 +164,58 @@
         ],
         compiler_params=PARAMS,
         name="polar",
-    )(*grams)
-
-
-def rotate_kernel(whole, last, flag_ref, *refs):
-    if whole:
-        x_ref, q_ref, *outs = refs
-        pairs = [x_ref[:, : 2 * B], x_ref[:, 2 * B :]]
-    else:
-        t0_ref, b0_ref, t1_ref, b1_ref, q_ref, *outs = refs
-        pairs = [beside(t0_ref[...], b0_ref[...]), beside(t1_ref[...], b1_ref[...])]
-    turned = [dot3(halves(pairs[k]), halves(q_ref[k])) for k in range(2)]
-    if last:
-        outs[0][:, : 2 * B] = turned[0]
-        outs[0][:, 2 * B :] = turned[1]
-        return
-    right_ref, left_ref, t1n_ref, b0n_ref = outs
-    first = flag_ref[0] == 1
-    t0, b0 = turned[0][:, :B], turned[0][:, B:]
-    right_ref[...] = turned[1][:, :B]
-    left_ref[...] = jnp.where(first, t0, b0)
-    t1n_ref[...] = jnp.where(first, b0, t0)
-    b0n_ref[...] = turned[1][:, B:]
-
-
-def rotate(flags, blocks, q, last=False, rows=None, start=0):
-    whole = len(blocks) == 1
-    rows = rows or blocks[0].shape[0]
-    tile = min(TILE, rows)
-    offset = start // tile
+    )(flags, *grams)
+
+
+def rotate_kernel(t0_ref, b0_ref, t1_ref, b1_ref, q_ref, *outs):
+    for pair, (top_ref, bottom_ref) in enumerate(((t0_ref, b0_ref), (t1_ref, b1_ref))):
+        turned = dot3(halves(beside(top_ref[...], bottom_ref[...])), halves(q_ref[pair]))
+        if len(outs) == 1:
+            outs[0][:, 2 * B * pair : 2 * B * (pair + 1)] = turned
+        else:
+            outs[2 * pair][...] = turned[:, :B]
+            outs[2 * pair + 1][...] = turned[:, B:]
+
+
+def rotate(blocks, q, last=False):
+    rows = blocks[0].shape[0]
+    tile = min(TILE, rows)
     block = pl.BlockSpec((tile, B), lambda i: (i, 0))
-    wide = pl.BlockSpec((tile, 4 * B), lambda i: (i + offset, 0))
     full = pl.BlockSpec((2, 2 * B, 2 * B), lambda i: (0, 0, 0))
     if last:
-        out_specs, out_shape = wide, jax.ShapeDtypeStruct((rows, 4 * B), F32)
+        out_specs, out_shape = pl.BlockSpec((tile, 4 * B), lambda i: (i, 0)), jax.ShapeDtypeStruct((rows, 4 * B), F32)
     else:
         out_specs, out_shape = [block] * 4, [jax.ShapeDtypeStruct((rows, B), F32)] * 4
     return pl.pallas_call(
-        functools.partial(rotate_kernel, whole, last),
-        grid=(rows // tile,),
-        in_specs=[pl.BlockSpec(memory_space=pltpu.SMEM)] + ([wide] if whole else [block] * 4) + [full],
+        rotate_kernel,
+        grid=(rows // tile,),
+        in_specs=[block] * 4 + [full],
         out_specs=out_specs,
         out_shape=out_shape,
         compiler_params=PARAMS,
         name="rotate",
-    )(flags, *blocks, q)
+    )(*blocks, q)
+
+
+def rotate_part_kernel(columns, x_ref, q_ref, *outs):
+    for pair in range(2):
+        q = halves(q_ref[pair, :, columns[pair] : columns[pair] + B])
+        outs[pair][...] = dot3_narrow(halves(x_ref[:, 2 * B * pair : 2 * B * (pair + 1)]), q)
+
+
+def rotate_part(x, q, columns):
+    rows = x.shape[0]
+    tile = min(TILE, rows)
+    block = pl.BlockSpec((tile, B), lambda i: (i, 0))
+    return pl.pallas_call(
+        functools.partial(rotate_part_kernel, columns),
+        grid=(rows // tile,),
+        in_specs=[pl.BlockSpec((tile, 4 * B), lambda i: (i, 0)), pl.BlockSpec((2, 2 * B, 2 * B), lambda i: (0, 0, 0))],
+        out_specs=[block] * 2,
+        out_shape=[jax.ShapeDtypeStruct((rows, B), F32)] * 2,
+        compiler_params=PARAMS,
+        name="rotate_part",
+    )(x, q)
 
 
 def shifted(value, steps):
@@ -231,21 +247,22 @@
     flags = jnp.stack([position == 0, position == lax.axis_size("pair") - 1]).astype(jnp.int32)
     zero = jnp.zeros((2, GROWS, B), F32)
 
-    q, _, _ = polar(row_terms(gram_first(factor), False))
-    right, left, t1, b0 = rotate(flags, [factor], q)
+    q, _, _ = polar(flags, row_terms(gram_first(factor), False))
+    left, right = rotate_part(factor, q, (B, 0))
     arrived = (shifted(right, 1), shifted(left, -1))
+    t1, b0 = rotate_part(factor, q, (0, B))
     (t1, b0), arrived = after((t1, b0), arrived)
     ahead = (shifted(t1, 1), shifted(b0, -1))
     previous = (left, right)
     rebuilt = ()
     for step in range(1, STEPS):
         g, t0, b1 = gram_next(flags, (left, right, b0, t1, *arrived), rebuilt, zero)
-        q, q_right, q_left = polar(row_terms(g, step < STEPS - 1))
+        q, q_right, q_left = polar(flags, row_terms(g, step < STEPS - 1), step < STEPS - 1)
         if step == STEPS - 1:
-            return rotate(flags, [t0, b0, t1, b1], q, last=True)
+            return rotate([t0, b0, t1, b1], q, last=True)
         q_top, q_bottom = shifted(q_right, 1), shifted(q_left, -1)
         older = previous
-        right, left, t1, b0 = rotate(flags, [t0, b0, t1, b1], q)
+        t1, left, right, b0 = rotate([t0, b0, t1, b1], q)
         previous = (left, right)
         rebuilt = (*older, q_top, q_bottom)
         arrived = ahead

time: 240 us -> 224 us (0.933)
  Pallas kernels: 94.8 us -> 62.7 us
  waiting for transfers between devices: 81.3 us -> 98.3 us
    pallas_call x8 -> x9, Pallas kernels: 65.4 us -> 46.7 us  [the longest x4 27.2 us: polar(): pl.pallas_call(functools.partial(polar_kernel, swap), in_specs=[pl.BlockS...]
    ppermute x10, waiting for transfers between devices: 61.5 us -> 78.8 us  [shifted(): lax.ppermute(value, 'pair', [(source, source + steps) for source in range...]
    pallas_call x3, Pallas kernels: 26 us -> 13.5 us  [gram_next(): pl.pallas_call(functools.partial(gram_next_kernel, bool(rebuilt)), grid=(...]
    unnamed x26 -> x4, local copies, waits for them, and re-layouts: 7.44 us -> 6.76 us
  transfers between devices with their start and end apart: 22 -> 22, of which waited for: 13 -> 14; matrix products, arithmetic and copies ran while one was open for 0% -> 0% of each run, Pallas kernels for 20% -> 14%
where the time goes in v3:
time: 224 us
  waiting for transfers between devices  98.3 us (44%)
  Pallas kernels  62.7 us (28%)
  starting transfers between devices  55.3 us (25%)
  local copies, waits for them, and re-layouts  6.77 us (3%)
    ppermute x10, waiting for transfers between devices, shifted(): lax.ppermute(value, 'pair', [(source, source + steps) for source in range...  78.8 us
    ppermute x10, starting transfers between devices, shifted(): lax.ppermute(value, 'pair', [(source, source + steps) for source in range...  32.9 us
    pallas_call x4, Pallas kernels, polar(): pl.pallas_call(functools.partial(polar_kernel, swap), in_specs=[pl.BlockS...  27.2 us
    pallas_call x3, Pallas kernels, rotate(): pl.pallas_call(rotate_kernel, grid=(rows // tile,), in_specs=[block] * 4...  13.8 us
    pallas_call x3, Pallas kernels, gram_next(): pl.pallas_call(functools.partial(gram_next_kernel, bool(rebuilt)), grid=(...  13.5 us
    ppermute x2, starting transfers between devices, row_terms(): direct = lax.ppermute(part, both, [(i, i ^ 2) for i in here])  11 us
    ppermute x2, starting transfers between devices, row_terms(): return [part, lax.ppermute(part, 'row', [(r, r ^ 2) for r in range(rows)])]  7.98 us
    ppermute x2, waiting for transfers between devices, row_terms(): return [part, lax.ppermute(part, 'row', [(r, r ^ 2) for r in range(rows)])]  7.89 us
  transfers between devices with their start and end apart: 22, of which 14 were waited for; matrix products, arithmetic and copies ran while one was open for 0% of the time, Pallas kernels for 14%

profile of v3, /device:TPU:30, one launch (start us, length us, event | category | flops | bytes accessed | tf_op | source)
XLA Modules:
  0.0 223.5 jit_solution(12971496895555210954)
XLA Ops:
  7.4 4.0 %collective-permute-start.1 = (f32[2,136,128]{2,1,0:T(8,128)S(1)}, f32[2,136,128]{2,1,0:T(8,128)S(1)}, u32[]{:S(2)}, u32[]{:S(2)}) collective-permute-start(f32[2,136,128]{2,1,0:T(8,128)S(1)} %add.12.refs_0_), channel_id=1, source_target_pairs={{0,2},{1,3},{2,0},{3,1},{4,6},{5,7},{6,4},{7,5},{8,10},{9,11},{10,... | collective-permute-start | bytes 417800 | tf_op jit(solution)/shard_map/ppermute | solution.py:231
  15.3 7.1 %polar.4 = (f32[2,256,256]{2,1,0:T(8,128)S(1)}, f32[256,128]{1,0:T(8,128)}, f32[256,128]{1,0:T(8,128)}) custom-call(s32[2]{0:T(128)S(1)} %add_convert_fusion.flag_ref, f32[2,136,128]{2,1,0:T(8,128)S(1)} %add.12.refs_0_, f32[2,136,128]{2,1,0:T(8,128)S(1)} %collective-permute-done.1.refs_1_), custom_call_target="tpu_custom_call" | custom-call | tf_op jit(solution)/shard_map/polar/pallas_call | solution.py:157
  37.5 40.3 %collective-permute-done.2.in_top_ref = f32[4096,128]{1,0:T(8,128)S(1)} collective-permute-done((f32[4096,128]{1,0:T(8,128)S(1)}, f32[4096,128]{1,0:T(8,128)S(1)}, u32[]{:S(2)}, u32[]{:S(2)}) %collective-permute-start.2) | collective-permute-done | bytes 2097184 | tf_op jit(solution)/shard_map/ppermute | solution.py:224
  77.8 6.4 %collective-permute-done.3.in_bottom_ref = f32[4096,128]{1,0:T(8,128)S(1)} collective-permute-done((f32[4096,128]{1,0:T(8,128)S(1)}, f32[4096,128]{1,0:T(8,128)S(1)}, u32[]{:S(2)}, u32[]{:S(2)}) %collective-permute-start.3) | collective-permute-done | bytes 2097184 | tf_op jit(solution)/shard_map/ppermute | solution.py:224
  86.1 3.9 %collective-permute-start.9 = (f32[4096,128]{1,0:T(8,128)S(1)}, f32[4096,128]{1,0:T(8,128)S(1)}, u32[]{:S(2)}, u32[]{:S(2)}) collective-permute-start(f32[4096,128]{1,0:T(8,128)S(1)} %get-tuple-element.51.b0_ref), channel_id=1, source_target_pairs={{4,0},{8,4},{12,8},{16,12},{20,16},{24,20},{28,24},{32,28},{36,32}... | collective-permute-start | bytes 6291464 | tf_op jit(solution)/shard_map/ppermute | solution.py:224
  95.5 5.5 %collective-permute-start.5 = (f32[2,136,128]{2,1,0:T(8,128)S(1)}, f32[2,136,128]{2,1,0:T(8,128)S(1)}, u32[]{:S(2)}, u32[]{:S(2)}) collective-permute-start(f32[2,136,128]{2,1,0:T(8,128)S(1)} %add.13.refs_0_), channel_id=1, source_target_pairs={{4,6},{5,7},{6,4},{7,5},{8,10},{9,11},{10,8},{11,9},{12,14},{13,15... | collective-permute-start | bytes 417800 | tf_op jit(solution)/shard_map/ppermute | solution.py:237
  105.0 6.5 %polar.5 = (f32[2,256,256]{2,1,0:T(8,128)S(1)}, f32[256,128]{1,0:T(8,128)S(1)}, f32[256,128]{1,0:T(8,128)S(1)}) custom-call(s32[2]{0:T(128)S(1)} %add_convert_fusion.flag_ref, f32[2,136,128]{2,1,0:T(8,128)S(1)} %add.13.refs_0_, f32[2,136,128]{2,1,0:T(8,128)S(1)} %collective-permute-done.5.refs_1_, f32[2,136,128]{2,1,0:T(8,128)S(1)} %collective-permute-done.7.refs_2_), custom_call_target="tpu_custom_call" | custom-call | tf_op jit(solution)/shard_map/polar/pallas_call | solution.py:157
  111.4 5.8 %collective-permute-start.10 = (f32[256,128]{1,0:T(8,128)S(1)}, f32[256,128]{1,0:T(8,128)S(1)}, u32[]{:S(2)}, u32[]{:S(2)}) collective-permute-start(f32[256,128]{1,0:T(8,128)S(1)} %get-tuple-element.63), channel_id=1, source_target_pairs={{0,4},{4,8},{8,12},{12,16},{16,20},{20,24},{24,28},{28,32},{32,36}... | collective-permute-start | bytes 393224 | tf_op jit(solution)/shard_map/ppermute | solution.py:224
  119.2 4.0 %rotate.3 = (f32[4096,128]{1,0:T(8,128)S(1)}, f32[4096,128]{1,0:T(8,128)S(1)}, f32[4096,128]{1,0:T(8,128)S(1)}, f32[4096,128]{1,0:T(8,128)S(1)}) custom-call(f32[4096,128]{1,0:T(8,128)S(1)} %get-tuple-element.55.t0_ref, f32[4096,128]{1,0:T(8,128)S(1)} %get-tuple-element.51.b0_ref, f32[4096,128]{1,0:T(8,128)S(1)} %get-tuple-element.52.t1_ref, ...), custom_call_target="tpu_custom_call" | custom-call | tf_op jit(solution)/shard_map/rotate/pallas_call | solution.py:189
  123.2 11.3 %collective-permute-done.10.rest_2_ = f32[256,128]{1,0:T(8,128)S(1)} collective-permute-done((f32[256,128]{1,0:T(8,128)S(1)}, f32[256,128]{1,0:T(8,128)S(1)}, u32[]{:S(2)}, u32[]{:S(2)}) %collective-permute-start.10) | collective-permute-done | bytes 131104 | tf_op jit(solution)/shard_map/ppermute | solution.py:224
  134.5 6.1 %collective-permute-done.11.rest_3_ = f32[256,128]{1,0:T(8,128)S(1)} collective-permute-done((f32[256,128]{1,0:T(8,128)S(1)}, f32[256,128]{1,0:T(8,128)S(1)}, u32[]{:S(2)}, u32[]{:S(2)}) %collective-permute-start.11) | collective-permute-done | bytes 131104 | tf_op jit(solution)/shard_map/ppermute | solution.py:224
  142.6 3.9 %collective-permute-start.17 = (f32[4096,128]{1,0:T(8,128)S(1)}, f32[4096,128]{1,0:T(8,128)S(1)}, u32[]{:S(2)}, u32[]{:S(2)}) collective-permute-start(f32[4096,128]{1,0:T(8,128)S(1)} %get-tuple-element.65.b0_ref), channel_id=1, source_target_pairs={{4,0},{8,4},{12,8},{16,12},{20,16},{24,20},{28,24},{32,28},{36,32}... | collective-permute-start | bytes 6291464 | tf_op jit(solution)/shard_map/ppermute | solution.py:224
  146.5 5.1 %gram_next.4 = (f32[2,136,128]{2,1,0:T(8,128)S(1)}, f32[4096,128]{1,0:T(8,128)S(1)}, f32[4096,128]{1,0:T(8,128)S(1)}) custom-call(s32[2]{0:T(128)S(1)} %add_convert_fusion.flag_ref, f32[4096,128]{1,0:T(8,128)S(1)} %get-tuple-element.59.first_ref.rest_0_, f32[4096,128]{1,0:T(8,128)S(1)} %get-tuple-element.60.last_ref.rest_1_, ...), custom_call_target="tpu_custom_call" | custom-call | tf_op jit(solution)/shard_map/gram_next/pallas_call | solution.py:107
  153.7 5.5 %collective-permute-start.13 = (f32[2,136,128]{2,1,0:T(8,128)S(1)}, f32[2,136,128]{2,1,0:T(8,128)S(1)}, u32[]{:S(2)}, u32[]{:S(2)}) collective-permute-start(f32[2,136,128]{2,1,0:T(8,128)S(1)} %add.14.refs_0_), channel_id=1, source_target_pairs={{4,6},{5,7},{6,4},{7,5},{8,10},{9,11},{10,8},{11,9},{12,14},{13,15... | collective-permute-start | bytes 417800 | tf_op jit(solution)/shard_map/ppermute | solution.py:237
  163.2 6.5 %polar.6 = (f32[2,256,256]{2,1,0:T(8,128)S(1)}, f32[256,128]{1,0:T(8,128)S(1)}, f32[256,128]{1,0:T(8,128)S(1)}) custom-call(s32[2]{0:T(128)S(1)} %add_convert_fusion.flag_ref, f32[2,136,128]{2,1,0:T(8,128)S(1)} %add.14.refs_0_, f32[2,136,128]{2,1,0:T(8,128)S(1)} %collective-permute-done.13.refs_1_, f32[2,136,128]{2,1,0:T(8,128)S(1)} %collective-permute-done.15.refs_2_), custom_call_target="tpu_custom_call" | custom-call | tf_op jit(solution)/shard_map/polar/pallas_call | solution.py:157
  169.7 5.8 %collective-permute-start.18 = (f32[256,128]{1,0:T(8,128)S(1)}, f32[256,128]{1,0:T(8,128)S(1)}, u32[]{:S(2)}, u32[]{:S(2)}) collective-permute-start(f32[256,128]{1,0:T(8,128)S(1)} %get-tuple-element.81), channel_id=1, source_target_pairs={{0,4},{4,8},{8,12},{12,16},{16,20},{20,24},{24,28},{28,32},{32,36}... | collective-permute-start | bytes 393224 | tf_op jit(solution)/shard_map/ppermute | solution.py:224
  177.4 4.1 %rotate.4 = (f32[4096,128]{1,0:T(8,128)S(1)}, f32[4096,128]{1,0:T(8,128)S(1)}, f32[4096,128]{1,0:T(8,128)S(1)}, f32[4096,128]{1,0:T(8,128)S(1)}) custom-call(f32[4096,128]{1,0:T(8,128)S(1)} %get-tuple-element.73.t0_ref, f32[4096,128]{1,0:T(8,128)S(1)} %get-tuple-element.65.b0_ref, f32[4096,128]{1,0:T(8,128)S(1)} %get-tuple-element.66.t1_ref, ...), custom_call_target="tpu_custom_call" | custom-call | tf_op jit(solution)/shard_map/rotate/pallas_call | solution.py:189
  181.5 8.6 %collective-permute-done.18.rest_2_ = f32[256,128]{1,0:T(8,128)S(1)} collective-permute-done((f32[256,128]{1,0:T(8,128)S(1)}, f32[256,128]{1,0:T(8,128)S(1)}, u32[]{:S(2)}, u32[]{:S(2)}) %collective-permute-start.18) | collective-permute-done | bytes 131104 | tf_op jit(solution)/shard_map/ppermute | solution.py:224
  190.1 6.1 %collective-permute-done.19.rest_3_ = f32[256,128]{1,0:T(8,128)S(1)} collective-permute-done((f32[256,128]{1,0:T(8,128)S(1)}, f32[256,128]{1,0:T(8,128)S(1)}, u32[]{:S(2)}, u32[]{:S(2)}) %collective-permute-start.19) | collective-permute-done | bytes 131104 | tf_op jit(solution)/shard_map/ppermute | solution.py:224
  196.2 5.1 %gram_next.5 = (f32[2,136,128]{2,1,0:T(8,128)S(1)}, f32[4096,128]{1,0:T(8,128)S(1)}, f32[4096,128]{1,0:T(8,128)S(1)}) custom-call(s32[2]{0:T(128)S(1)} %add_convert_fusion.flag_ref, f32[4096,128]{1,0:T(8,128)S(1)} %get-tuple-element.77.first_ref, f32[4096,128]{1,0:T(8,128)S(1)} %get-tuple-element.78.last_ref, f32[4096,128]{1,0:T(8,128)S(1)} %get-tuple-element.79.b0_ref, ...), custom_call_target="tpu_custom_call" | custom-call | tf_op jit(solution)/shard_map/gram_next/pallas_call | solution.py:107
  202.8 4.0 %collective-permute-start.21 = (f32[2,136,128]{2,1,0:T(8,128)S(1)}, f32[2,136,128]{2,1,0:T(8,128)S(1)}, u32[]{:S(2)}, u32[]{:S(2)}) collective-permute-start(f32[2,136,128]{2,1,0:T(8,128)S(1)} %add.15.refs_0_), channel_id=1, source_target_pairs={{0,2},{1,3},{2,0},{3,1},{4,6},{5,7},{6,4},{7,5},{8,10},{9,11},{10,... | collective-permute-start | bytes 417800 | tf_op jit(solution)/shard_map/ppermute | solution.py:231
  206.8 4.0 %collective-permute-done.21.refs_1_ = f32[2,136,128]{2,1,0:T(8,128)S(1)} collective-permute-done((f32[2,136,128]{2,1,0:T(8,128)S(1)}, f32[2,136,128]{2,1,0:T(8,128)S(1)}, u32[]{:S(2)}, u32[]{:S(2)}) %collective-permute-start.21) | collective-permute-done | bytes 139296 | tf_op jit(solution)/shard_map/ppermute | solution.py:231
  210.8 7.1 %polar.7 = (f32[2,256,256]{2,1,0:T(8,128)S(1)}, f32[256,128]{1,0:T(8,128)}, f32[256,128]{1,0:T(8,128)}) custom-call(s32[2]{0:T(128)S(1)} %add_convert_fusion.flag_ref, f32[2,136,128]{2,1,0:T(8,128)S(1)} %add.15.refs_0_, f32[2,136,128]{2,1,0:T(8,128)S(1)} %collective-permute-done.21.refs_1_), custom_call_target="tpu_custom_call" | custom-call | tf_op jit(solution)/shard_map/polar/pallas_call | solution.py:157
  217.9 5.6 %rotate.5 = f32[4096,512]{1,0:T(8,128)} custom-call(f32[4096,128]{1,0:T(8,128)S(1)} %get-tuple-element.83.t0_ref, f32[4096,128]{1,0:T(8,128)S(1)} %get-tuple-element.79.b0_ref, f32[4096,128]{1,0:T(8,128)S(1)} %get-tuple-element.80.t1_ref, f32[4096,128]{1,0:T(8,128)S(1)} %get-tuple-element.84.b1_ref, f32[2,256,256]{2,1,0:T(8,128)S(1)} %get-tuple-element.86.q_ref), custom_call_target="tpu_custom_call" | custom-call | tf_op jit(solution)/shard_map/rotate/pallas_call | solution.py:189
  (43 shorter events, 51.0 us)
Async XLA Ops:
  0.0 3.4 %copy-start = (f32[4096,512]{1,0:T(8,128)S(1)}, f32[4096,512]{1,0:T(8,128)}, u32[]{:S(2)}) copy-start(f32[4096,512]{1,0:T(8,128)} %x_ref.5) | copy-start | bytes 25165828
  5.9 1.4 collective-permute-start
  7.4 7.9 %collective-permute-start.1 = (f32[2,136,128]{2,1,0:T(8,128)S(1)}, f32[2,136,128]{2,1,0:T(8,128)S(1)}, u32[]{:S(2)}, u32[]{:S(2)}) collective-permute-start(f32[2,136,128]{2,1,0:T(8,128)S(1)} %add.12.refs_0_), channel_id=1, source_target_pairs={{0,2},{1,3},{2,0},{3,1},{4,6},{5,7},{6,4},{7,5},{8,10},{9,11},{10,... | collective-permute-start | bytes 417800 | tf_op jit(solution)/shard_map/ppermute | solution.py:231
  22.4 3.4 %copy-start.1 = (f32[4096,512]{1,0:T(8,128)S(1)}, f32[4096,512]{1,0:T(8,128)}, u32[]{:S(2)}) copy-start(f32[4096,512]{1,0:T(8,128)} %x_ref.5) | copy-start | bytes 25165828
  28.7 49.1 %collective-permute-start.2 = (f32[4096,128]{1,0:T(8,128)S(1)}, f32[4096,128]{1,0:T(8,128)S(1)}, u32[]{:S(2)}, u32[]{:S(2)}) collective-permute-start(f32[4096,128]{1,0:T(8,128)S(1)} %get-tuple-element.70.last_ref.rest_1_), channel_id=1, source_target_pairs={{0,4},{4,8},{8,12},{12,16},{16,20},{20,24},{24,28},{28,32},{32,36}... | collective-permute-start | bytes 6291464 | tf_op jit(solution)/shard_map/ppermute | solution.py:224
  31.5 52.7 %collective-permute-start.3 = (f32[4096,128]{1,0:T(8,128)S(1)}, f32[4096,128]{1,0:T(8,128)S(1)}, u32[]{:S(2)}, u32[]{:S(2)}) collective-permute-start(f32[4096,128]{1,0:T(8,128)S(1)} %get-tuple-element.69.first_ref.rest_0_), channel_id=1, source_target_pairs={{4,0},{8,4},{12,8},{16,12},{20,16},{24,20},{28,24},{32,28},{36,32}... | collective-permute-start | bytes 6291464 | tf_op jit(solution)/shard_map/ppermute | solution.py:224
  84.2 56.5 %collective-permute-start.8 = (f32[4096,128]{1,0:T(8,128)S(1)}, f32[4096,128]{1,0:T(8,128)S(1)}, u32[]{:S(2)}, u32[]{:S(2)}) collective-permute-start(f32[4096,128]{1,0:T(8,128)S(1)} %get-tuple-element.52.t1_ref), channel_id=1, source_target_pairs={{0,4},{4,8},{8,12},{12,16},{16,20},{20,24},{24,28},{28,32},{32,36}... | collective-permute-start | bytes 6291464 | tf_op jit(solution)/shard_map/ppermute | solution.py:224
  86.1 54.6 %collective-permute-start.9 = (f32[4096,128]{1,0:T(8,128)S(1)}, f32[4096,128]{1,0:T(8,128)S(1)}, u32[]{:S(2)}, u32[]{:S(2)}) collective-permute-start(f32[4096,128]{1,0:T(8,128)S(1)} %get-tuple-element.51.b0_ref), channel_id=1, source_target_pairs={{4,0},{8,4},{12,8},{16,12},{20,16},{24,20},{28,24},{32,28},{36,32}... | collective-permute-start | bytes 6291464 | tf_op jit(solution)/shard_map/ppermute | solution.py:224
  93.4 1.4 collective-permute-start.4
  94.8 6.2 %collective-permute-start.6 = (f32[2,136,128]{2,1,0:T(8,128)S(1)}, f32[2,136,128]{2,1,0:T(8,128)S(1)}, u32[]{:S(2)}, u32[]{:S(2)}) collective-permute-start(f32[2,136,128]{2,1,0:T(8,128)S(1)} %add.13.refs_0_), channel_id=1, source_target_pairs={{0,22},{1,23},{2,20},{3,21},{124,106},{125,107},{126,104},{127,105}} | collective-permute-start | bytes 417800 | tf_op jit(solution)/shard_map/ppermute | solution.py:236
  95.5 9.5 %collective-permute-start.5 = (f32[2,136,128]{2,1,0:T(8,128)S(1)}, f32[2,136,128]{2,1,0:T(8,128)S(1)}, u32[]{:S(2)}, u32[]{:S(2)}) collective-permute-start(f32[2,136,128]{2,1,0:T(8,128)S(1)} %add.13.refs_0_), channel_id=1, source_target_pairs={{4,6},{5,7},{6,4},{7,5},{8,10},{9,11},{10,8},{11,9},{12,14},{13,15... | collective-permute-start | bytes 417800 | tf_op jit(solution)/shard_map/ppermute | solution.py:237
  101.0 4.0 %collective-permute-start.7 = (f32[2,136,128]{2,1,0:T(8,128)S(1)}, f32[2,136,128]{2,1,0:T(8,128)S(1)}, u32[]{:S(2)}, u32[]{:S(2)}) collective-permute-start(f32[2,136,128]{2,1,0:T(8,128)S(1)} %collective-permute-done.6), channel_id=1, source_target_pairs={{20,0},{21,1},{22,2},{23,3},{104,124},{105,125},{106,126},{107,127}} | collective-permute-start | bytes 417800 | tf_op jit(solution)/shard_map/ppermute | solution.py:238
  111.4 23.1 %collective-permute-start.10 = (f32[256,128]{1,0:T(8,128)S(1)}, f32[256,128]{1,0:T(8,128)S(1)}, u32[]{:S(2)}, u32[]{:S(2)}) collective-permute-start(f32[256,128]{1,0:T(8,128)S(1)} %get-tuple-element.63), channel_id=1, source_target_pairs={{0,4},{4,8},{8,12},{12,16},{16,20},{20,24},{24,28},{28,32},{32,36}... | collective-permute-start | bytes 393224 | tf_op jit(solution)/shard_map/ppermute | solution.py:224
  117.2 23.4 %collective-permute-start.11 = (f32[256,128]{1,0:T(8,128)S(1)}, f32[256,128]{1,0:T(8,128)S(1)}, u32[]{:S(2)}, u32[]{:S(2)}) collective-permute-start(f32[256,128]{1,0:T(8,128)S(1)} %get-tuple-element.64), channel_id=1, source_target_pairs={{4,0},{8,4},{12,8},{16,12},{20,16},{24,20},{28,24},{32,28},{36,32}... | collective-permute-start | bytes 393224 | tf_op jit(solution)/shard_map/ppermute | solution.py:224
  140.7 55.6 %collective-permute-start.16 = (f32[4096,128]{1,0:T(8,128)S(1)}, f32[4096,128]{1,0:T(8,128)S(1)}, u32[]{:S(2)}, u32[]{:S(2)}) collective-permute-start(f32[4096,128]{1,0:T(8,128)S(1)} %get-tuple-element.66.t1_ref), channel_id=1, source_target_pairs={{0,4},{4,8},{8,12},{12,16},{16,20},{20,24},{24,28},{28,32},{32,36}... | collective-permute-start | bytes 6291464 | tf_op jit(solution)/shard_map/ppermute | solution.py:224
  142.6 53.7 %collective-permute-start.17 = (f32[4096,128]{1,0:T(8,128)S(1)}, f32[4096,128]{1,0:T(8,128)S(1)}, u32[]{:S(2)}, u32[]{:S(2)}) collective-permute-start(f32[4096,128]{1,0:T(8,128)S(1)} %get-tuple-element.65.b0_ref), channel_id=1, source_target_pairs={{4,0},{8,4},{12,8},{16,12},{20,16},{24,20},{28,24},{32,28},{36,32}... | collective-permute-start | bytes 6291464 | tf_op jit(solution)/shard_map/ppermute | solution.py:224
  151.6 1.4 collective-permute-start.12
  153.1 6.2 %collective-permute-start.14 = (f32[2,136,128]{2,1,0:T(8,128)S(1)}, f32[2,136,128]{2,1,0:T(8,128)S(1)}, u32[]{:S(2)}, u32[]{:S(2)}) collective-permute-start(f32[2,136,128]{2,1,0:T(8,128)S(1)} %add.14.refs_0_), channel_id=1, source_target_pairs={{0,22},{1,23},{2,20},{3,21},{124,106},{125,107},{126,104},{127,105}} | collective-permute-start | bytes 417800 | tf_op jit(solution)/shard_map/ppermute | solution.py:236
  153.7 9.5 %collective-permute-start.13 = (f32[2,136,128]{2,1,0:T(8,128)S(1)}, f32[2,136,128]{2,1,0:T(8,128)S(1)}, u32[]{:S(2)}, u32[]{:S(2)}) collective-permute-start(f32[2,136,128]{2,1,0:T(8,128)S(1)} %add.14.refs_0_), channel_id=1, source_target_pairs={{4,6},{5,7},{6,4},{7,5},{8,10},{9,11},{10,8},{11,9},{12,14},{13,15... | collective-permute-start | bytes 417800 | tf_op jit(solution)/shard_map/ppermute | solution.py:237
  159.2 4.0 %collective-permute-start.15 = (f32[2,136,128]{2,1,0:T(8,128)S(1)}, f32[2,136,128]{2,1,0:T(8,128)S(1)}, u32[]{:S(2)}, u32[]{:S(2)}) collective-permute-start(f32[2,136,128]{2,1,0:T(8,128)S(1)} %collective-permute-done.14), channel_id=1, source_target_pairs={{20,0},{21,1},{22,2},{23,3},{104,124},{105,125},{106,126},{107,127}} | collective-permute-start | bytes 417800 | tf_op jit(solution)/shard_map/ppermute | solution.py:238
  169.7 20.4 %collective-permute-start.18 = (f32[256,128]{1,0:T(8,128)S(1)}, f32[256,128]{1,0:T(8,128)S(1)}, u32[]{:S(2)}, u32[]{:S(2)}) collective-permute-start(f32[256,128]{1,0:T(8,128)S(1)} %get-tuple-element.81), channel_id=1, source_target_pairs={{0,4},{4,8},{8,12},{12,16},{16,20},{20,24},{24,28},{28,32},{32,36}... | collective-permute-start | bytes 393224 | tf_op jit(solution)/shard_map/ppermute | solution.py:224
  175.5 20.8 %collective-permute-start.19 = (f32[256,128]{1,0:T(8,128)S(1)}, f32[256,128]{1,0:T(8,128)S(1)}, u32[]{:S(2)}, u32[]{:S(2)}) collective-permute-start(f32[256,128]{1,0:T(8,128)S(1)} %get-tuple-element.82), channel_id=1, source_target_pairs={{4,0},{8,4},{12,8},{16,12},{20,16},{24,20},{28,24},{32,28},{36,32}... | collective-permute-start | bytes 393224 | tf_op jit(solution)/shard_map/ppermute | solution.py:224
  201.3 1.4 collective-permute-start.20
  202.8 8.0 %collective-permute-start.21 = (f32[2,136,128]{2,1,0:T(8,128)S(1)}, f32[2,136,128]{2,1,0:T(8,128)S(1)}, u32[]{:S(2)}, u32[]{:S(2)}) collective-permute-start(f32[2,136,128]{2,1,0:T(8,128)S(1)} %add.15.refs_0_), channel_id=1, source_target_pairs={{0,2},{1,3},{2,0},{3,1},{4,6},{5,7},{6,4},{7,5},{8,10},{9,11},{10,... | collective-permute-start | bytes 417800 | tf_op jit(solution)/shard_map/ppermute | solution.py:231

commit v4 on v3

--- a/solution.py
+++ b/solution.py
@@ -13,10 +13,13 @@
 DAMPING = 0.04
 TILE = 1024
 GROWS = 136
+LOADS = 4
 RELAY = 5
 F32 = jnp.float32
 BF16 = jnp.bfloat16
-PARAMS = pltpu.CompilerParams(vmem_limit_bytes=24 * 1024 * 1024)
+LONG = pl.CostEstimate(flops=60 * 10**9, bytes_accessed=1 << 20, transcendentals=0)
+SHORT = pl.CostEstimate(flops=5 * 10**9, bytes_accessed=1 << 20, transcendentals=0)
+PARAMS = pltpu.CompilerParams(vmem_limit_bytes=20 * 1024 * 1024)
 NN = (((1,), (0,)), ((), ()))
 NT = (((1,), (1,)), ((), ()))
 TN = (((0,), (0,)), ((), ()))
@@ -51,26 +54,31 @@
     g_ref[pair, B + 1 : B + 2, :] += jnp.sum(bottom * bottom, axis=0, keepdims=True)
 
 
-def gram_first_kernel(x_ref, g_ref):
-    @pl.when(pl.program_id(0) == 0)
-    def _():
-        g_ref[...] = jnp.zeros_like(g_ref)
-
-    for pair in range(2):
-        base = 2 * B * pair
-        add_gram(g_ref, pair, x_ref[:, base : base + B], x_ref[:, base + B : base + 2 * B])
+def gram_first_kernel(x_ref, copy_ref, g_ref, sems):
+    tile = x_ref.shape[0] // LOADS
+    loads = []
+    for i in range(LOADS):
+        rows = pl.ds(i * tile, tile)
+        loads.append(pltpu.make_async_copy(x_ref.at[rows], copy_ref.at[rows], sems.at[i]))
+        loads[-1].start()
+    g_ref[...] = jnp.zeros_like(g_ref)
+    for i in range(LOADS):
+        loads[i].wait()
+        for pair in range(2):
+            base = 2 * B * pair
+            rows = slice(i * tile, (i + 1) * tile)
+            add_gram(g_ref, pair, copy_ref[rows, base : base + B], copy_ref[rows, base + B : base + 2 * B])
 
 
 def gram_first(x):
-    rows = x.shape[0]
-    tile = min(TILE, rows)
+    vmem = pl.BlockSpec(memory_space=pltpu.VMEM)
     return pl.pallas_call(
         gram_first_kernel,
-        grid=(rows // tile,),
-        in_specs=[pl.BlockSpec((tile, 4 * B), lambda i: (i, 0))],
-        out_specs=pl.BlockSpec((2, GROWS, B), lambda i: (0, 0, 0)),
-        out_shape=jax.ShapeDtypeStruct((2, GROWS, B), F32),
-        compiler_params=PARAMS,
+        in_specs=[pl.BlockSpec(memory_space=pl.ANY)],
+        out_specs=[vmem, vmem],
+        out_shape=[jax.ShapeDtypeStruct(x.shape, F32), jax.ShapeDtypeStruct((2, GROWS, B), F32)],
+        scratch_shapes=[pltpu.SemaphoreType.DMA((LOADS,))],
+        compiler_params=pltpu.CompilerParams(vmem_limit_bytes=40 * 1024 * 1024),
         name="gram_first",
     )(x)
 
@@ -111,6 +119,7 @@
         out_specs=[gram, block, block],
         out_shape=[jax.ShapeDtypeStruct((2, GROWS, B), F32)] + [jax.ShapeDtypeStruct((rows, B), F32)] * 2,
         compiler_params=PARAMS,
+        cost_estimate=LONG,
         name="gram_next",
     )(flags, *blocks, *rebuilt, g_in)
 
@@ -163,6 +172,7 @@
             jax.ShapeDtypeStruct((2 * B, B), F32),
         ],
         compiler_params=PARAMS,
+        cost_estimate=SHORT,
         name="polar",
     )(flags, *grams)
 
@@ -193,6 +203,7 @@
         out_specs=out_specs,
         out_shape=out_shape,
         compiler_params=PARAMS,
+        cost_estimate=SHORT,
         name="rotate",
     )(*blocks, q)
 
@@ -238,20 +249,16 @@
     return [part, direct, lax.ppermute(hop, both, [(via, end) for end, via in ends])]
 
 
-def after(values, done):
-    return lax.optimization_barrier((values, done))
-
-
 def per_device(factor):
     position = lax.axis_index("pair")
     flags = jnp.stack([position == 0, position == lax.axis_size("pair") - 1]).astype(jnp.int32)
     zero = jnp.zeros((2, GROWS, B), F32)
 
-    q, _, _ = polar(flags, row_terms(gram_first(factor), False))
+    factor, g = gram_first(factor)
+    q, _, _ = polar(flags, row_terms(g, False))
     left, right = rotate_part(factor, q, (B, 0))
     arrived = (shifted(right, 1), shifted(left, -1))
     t1, b0 = rotate_part(factor, q, (0, B))
-    (t1, b0), arrived = after((t1, b0), arrived)
     ahead = (shifted(t1, 1), shifted(b0, -1))
     previous = (left, right)
     rebuilt = ()
@@ -261,13 +268,11 @@
         if step == STEPS - 1:
             return rotate([t0, b0, t1, b1], q, last=True)
         q_top, q_bottom = shifted(q_right, 1), shifted(q_left, -1)
-        older = previous
+        rebuilt = (*previous, q_top, q_bottom)
         t1, left, right, b0 = rotate([t0, b0, t1, b1], q)
         previous = (left, right)
-        rebuilt = (*older, q_top, q_bottom)
         arrived = ahead
         if step < STEPS - 2:
-            (t1, b0), (arrived, rebuilt) = after((t1, b0), (arrived, rebuilt))
             ahead = (shifted(t1, 1), shifted(b0, -1))
 
 

time: 224 us -> 208 us (0.929); the launches traced: 224 us -> 205 us
  waiting for transfers between devices: 98.3 us -> 78.7 us
  local copies, waits for them, and re-layouts: 6.77 us -> 3.41 us
  starting transfers between devices: 55.3 us -> 58.1 us
    ppermute x10, waiting for transfers between devices: 78.8 us -> 59.3 us  [shifted(): lax.ppermute(value, 'pair', [(source, source + steps) for source in range...]
    unnamed x4, local copies, waits for them, and re-layouts: 6.76 us -> 3.4 us
    ppermute x10, starting transfers between devices: 32.9 us -> 35.2 us  [shifted(): lax.ppermute(value, 'pair', [(source, source + steps) for source in range...]
  transfers between devices with their start and end apart: 22 -> 22, of which waited for: 14 -> 15; matrix products, arithmetic and copies ran while one was open for 0% -> 0% of each run, Pallas kernels for 14% -> 16%
where the time goes in v4:
time: 208 us; the launch traced here: 205 us
  waiting for transfers between devices  78.7 us (38%)
  Pallas kernels  64.3 us (31%)
  starting transfers between devices  58.1 us (28%)
  local copies, waits for them, and re-layouts  3.41 us (2%)
    ppermute x10, waiting for transfers between devices, shifted(): lax.ppermute(value, 'pair', [(source, source + steps) for source in range...  59.3 us
    ppermute x10, starting transfers between devices, shifted(): lax.ppermute(value, 'pair', [(source, source + steps) for source in range...  35.2 us
    pallas_call x4, Pallas kernels, polar(): pl.pallas_call(functools.partial(polar_kernel, swap), in_specs=[pl.BlockS...  27.1 us
    pallas_call x3, Pallas kernels, rotate(): pl.pallas_call(rotate_kernel, grid=(rows // tile,), in_specs=[block] * 4...  13.8 us
    pallas_call x3, Pallas kernels, gram_next(): pl.pallas_call(functools.partial(gram_next_kernel, bool(rebuilt)), grid=(...  13.5 us
    ppermute x2, starting transfers between devices, row_terms(): direct = lax.ppermute(part, both, [(i, i ^ 2) for i in here])  11.7 us
    ppermute x2, waiting for transfers between devices, row_terms(): return [part, lax.ppermute(part, 'row', [(r, r ^ 2) for r in range(rows)])]  7.89 us
    ppermute x2, starting transfers between devices, row_terms(): return [part, lax.ppermute(part, 'row', [(r, r ^ 2) for r in range(rows)])]  7.88 us
  transfers between devices with their start and end apart: 22, of which 15 were waited for; matrix products, arithmetic and copies ran while one was open for 0% of the time, Pallas kernels for 16%

profile of v4, /device:TPU:30, one launch (start us, length us, event | category | flops | bytes accessed | tf_op | source)
XLA Modules:
  0.0 205.0 jit_solution(10020703818651012517)
XLA Ops:
  0.0 4.1 %gram_first.1 = (f32[4096,512]{1,0:T(8,128)S(1)}, f32[2,136,128]{2,1,0:T(8,128)S(1)}) custom-call(f32[4096,512]{1,0:T(8,128)} %x_ref.1), custom_call_target="tpu_custom_call" | custom-call | tf_op jit(solution)/shard_map/gram_first/pallas_call | solution.py:75
  8.9 4.0 %collective-permute-start.1 = (f32[2,136,128]{2,1,0:T(8,128)S(1)}, f32[2,136,128]{2,1,0:T(8,128)S(1)}, u32[]{:S(2)}, u32[]{:S(2)}) collective-permute-start(f32[2,136,128]{2,1,0:T(8,128)S(1)} %add.12.refs_0_), channel_id=1, source_target_pairs={{0,2},{1,3},{2,0},{3,1},{4,6},{5,7},{6,4},{7,5},{8,10},{9,11},{10,... | collective-permute-start | bytes 417800 | tf_op jit(solution)/shard_map/ppermute | solution.py:242
  12.9 3.9 %collective-permute-done.1.refs_1_ = f32[2,136,128]{2,1,0:T(8,128)S(1)} collective-permute-done((f32[2,136,128]{2,1,0:T(8,128)S(1)}, f32[2,136,128]{2,1,0:T(8,128)S(1)}, u32[]{:S(2)}, u32[]{:S(2)}) %collective-permute-start.1) | collective-permute-done | bytes 139296 | tf_op jit(solution)/shard_map/ppermute | solution.py:242
  16.9 7.1 %polar.4 = (f32[2,256,256]{2,1,0:T(8,128)S(1)}, f32[256,128]{1,0:T(8,128)}, f32[256,128]{1,0:T(8,128)}) custom-call(s32[2]{0:T(128)S(1)} %add_convert_fusion.flag_ref, f32[2,136,128]{2,1,0:T(8,128)S(1)} %add.12.refs_0_, f32[2,136,128]{2,1,0:T(8,128)S(1)} %collective-permute-done.1.refs_1_), custom_call_target="tpu_custom_call" | custom-call | flops 5000000000 | bytes 1048576 | tf_op jit(solution)/shard_map/polar/pallas_call | solution.py:166
  35.7 7.0 %collective-permute-start.8 = (f32[4096,128]{1,0:T(8,128)S(1)}, f32[4096,128]{1,0:T(8,128)S(1)}, u32[]{:S(2)}, u32[]{:S(2)}) collective-permute-start(f32[4096,128]{1,0:T(8,128)S(1)} %get-tuple-element.42.t1_ref), channel_id=1, source_target_pairs={{0,4},{4,8},{8,12},{12,16},{16,20},{20,24},{24,28},{28,32},{32,36}... | collective-permute-start | bytes 6291464 | tf_op jit(solution)/shard_map/ppermute | solution.py:235
  44.6 32.7 %collective-permute-done.2.in_top_ref = f32[4096,128]{1,0:T(8,128)S(1)} collective-permute-done((f32[4096,128]{1,0:T(8,128)S(1)}, f32[4096,128]{1,0:T(8,128)S(1)}, u32[]{:S(2)}, u32[]{:S(2)}) %collective-permute-start.2) | collective-permute-done | bytes 2097184 | tf_op jit(solution)/shard_map/ppermute | solution.py:235
  77.3 7.0 %collective-permute-done.3.in_bottom_ref = f32[4096,128]{1,0:T(8,128)S(1)} collective-permute-done((f32[4096,128]{1,0:T(8,128)S(1)}, f32[4096,128]{1,0:T(8,128)S(1)}, u32[]{:S(2)}, u32[]{:S(2)}) %collective-permute-start.3) | collective-permute-done | bytes 2097184 | tf_op jit(solution)/shard_map/ppermute | solution.py:235
  89.9 5.5 %collective-permute-start.5 = (f32[2,136,128]{2,1,0:T(8,128)S(1)}, f32[2,136,128]{2,1,0:T(8,128)S(1)}, u32[]{:S(2)}, u32[]{:S(2)}) collective-permute-start(f32[2,136,128]{2,1,0:T(8,128)S(1)} %add.13.refs_0_), channel_id=1, source_target_pairs={{4,6},{5,7},{6,4},{7,5},{8,10},{9,11},{10,8},{11,9},{12,14},{13,15... | collective-permute-start | bytes 417800 | tf_op jit(solution)/shard_map/ppermute | solution.py:248
  99.4 6.5 %polar.5 = (f32[2,256,256]{2,1,0:T(8,128)S(1)}, f32[256,128]{1,0:T(8,128)S(1)}, f32[256,128]{1,0:T(8,128)S(1)}) custom-call(s32[2]{0:T(128)S(1)} %add_convert_fusion.flag_ref, f32[2,136,128]{2,1,0:T(8,128)S(1)} %add.13.refs_0_, f32[2,136,128]{2,1,0:T(8,128)S(1)} %collective-permute-done.5.refs_1_, f32[2,136,128]{2,1,0:T(8,128)S(1)} %collective-permute-done.7.refs_2_), custom_call_target="tpu_custom_call" | custom-call | flops 5000000000 | bytes 1048576 | tf_op jit(solution)/shard_map/polar/pallas_call | solution.py:166
  107.8 3.9 %collective-permute-start.11 = (f32[256,128]{1,0:T(8,128)S(1)}, f32[256,128]{1,0:T(8,128)S(1)}, u32[]{:S(2)}, u32[]{:S(2)}) collective-permute-start(f32[256,128]{1,0:T(8,128)S(1)} %get-tuple-element.52), channel_id=1, source_target_pairs={{4,0},{8,4},{12,8},{16,12},{20,16},{24,20},{28,24},{32,28},{36,32}... | collective-permute-start | bytes 393224 | tf_op jit(solution)/shard_map/ppermute | solution.py:235
  111.7 4.1 %rotate.3 = (f32[4096,128]{1,0:T(8,128)S(1)}, f32[4096,128]{1,0:T(8,128)S(1)}, f32[4096,128]{1,0:T(8,128)S(1)}, f32[4096,128]{1,0:T(8,128)S(1)}) custom-call(f32[4096,128]{1,0:T(8,128)S(1)} %get-tuple-element.43.t0_ref, f32[4096,128]{1,0:T(8,128)S(1)} %get-tuple-element.41.b0_ref, f32[4096,128]{1,0:T(8,128)S(1)} %get-tuple-element.42.t1_ref, ...), custom_call_target="tpu_custom_call" | custom-call | flops 5000000000 | bytes 1048576 | tf_op jit(solution)/shard_map/rotate/pallas_call | solution.py:199
  115.8 6.1 %collective-permute-start.16 = (f32[4096,128]{1,0:T(8,128)S(1)}, f32[4096,128]{1,0:T(8,128)S(1)}, u32[]{:S(2)}, u32[]{:S(2)}) collective-permute-start(f32[4096,128]{1,0:T(8,128)S(1)} %get-tuple-element.50.t1_ref), channel_id=1, source_target_pairs={{0,4},{4,8},{8,12},{12,16},{16,20},{20,24},{24,28},{28,32},{32,36}... | collective-permute-start | bytes 6291464 | tf_op jit(solution)/shard_map/ppermute | solution.py:235
  130.4 5.0 %gram_next.4 = (f32[2,136,128]{2,1,0:T(8,128)S(1)}, f32[4096,128]{1,0:T(8,128)S(1)}, f32[4096,128]{1,0:T(8,128)S(1)}) custom-call(s32[2]{0:T(128)S(1)} %add_convert_fusion.flag_ref, f32[4096,128]{1,0:T(8,128)S(1)} %get-tuple-element.47.first_ref.rest_0_, f32[4096,128]{1,0:T(8,128)S(1)} %get-tuple-element.48.last_ref.rest_1_, ...), custom_call_target="tpu_custom_call" | custom-call | flops 60000002048 | bytes 1048576 | tf_op jit(solution)/shard_map/gram_next/pallas_call | solution.py:115
  137.5 6.2 %collective-permute-start.13 = (f32[2,136,128]{2,1,0:T(8,128)S(1)}, f32[2,136,128]{2,1,0:T(8,128)S(1)}, u32[]{:S(2)}, u32[]{:S(2)}) collective-permute-start(f32[2,136,128]{2,1,0:T(8,128)S(1)} %add.14.refs_0_), channel_id=1, source_target_pairs={{4,6},{5,7},{6,4},{7,5},{8,10},{9,11},{10,8},{11,9},{12,14},{13,15... | collective-permute-start | bytes 417800 | tf_op jit(solution)/shard_map/ppermute | solution.py:248
  147.7 6.5 %polar.6 = (f32[2,256,256]{2,1,0:T(8,128)S(1)}, f32[256,128]{1,0:T(8,128)S(1)}, f32[256,128]{1,0:T(8,128)S(1)}) custom-call(s32[2]{0:T(128)S(1)} %add_convert_fusion.flag_ref, f32[2,136,128]{2,1,0:T(8,128)S(1)} %add.14.refs_0_, f32[2,136,128]{2,1,0:T(8,128)S(1)} %collective-permute-done.13.refs_1_, f32[2,136,128]{2,1,0:T(8,128)S(1)} %collective-permute-done.15.refs_2_), custom_call_target="tpu_custom_call" | custom-call | flops 5000000000 | bytes 1048576 | tf_op jit(solution)/shard_map/polar/pallas_call | solution.py:166
  156.1 3.9 %collective-permute-start.19 = (f32[256,128]{1,0:T(8,128)S(1)}, f32[256,128]{1,0:T(8,128)S(1)}, u32[]{:S(2)}, u32[]{:S(2)}) collective-permute-start(f32[256,128]{1,0:T(8,128)S(1)} %get-tuple-element.62), channel_id=1, source_target_pairs={{4,0},{8,4},{12,8},{16,12},{20,16},{24,20},{28,24},{32,28},{36,32}... | collective-permute-start | bytes 393224 | tf_op jit(solution)/shard_map/ppermute | solution.py:235
  160.0 4.1 %rotate.4 = (f32[4096,128]{1,0:T(8,128)S(1)}, f32[4096,128]{1,0:T(8,128)S(1)}, f32[4096,128]{1,0:T(8,128)S(1)}, f32[4096,128]{1,0:T(8,128)S(1)}) custom-call(f32[4096,128]{1,0:T(8,128)S(1)} %get-tuple-element.53.t0_ref, f32[4096,128]{1,0:T(8,128)S(1)} %get-tuple-element.49.b0_ref, f32[4096,128]{1,0:T(8,128)S(1)} %get-tuple-element.50.t1_ref, ...), custom_call_target="tpu_custom_call" | custom-call | flops 5000000000 | bytes 1048576 | tf_op jit(solution)/shard_map/rotate/pallas_call | solution.py:199
  164.1 7.4 %collective-permute-done.18.rest_2_ = f32[256,128]{1,0:T(8,128)S(1)} collective-permute-done((f32[256,128]{1,0:T(8,128)S(1)}, f32[256,128]{1,0:T(8,128)S(1)}, u32[]{:S(2)}, u32[]{:S(2)}) %collective-permute-start.18) | collective-permute-done | bytes 131104 | tf_op jit(solution)/shard_map/ppermute | solution.py:235
  171.4 6.4 %collective-permute-done.19.rest_3_ = f32[256,128]{1,0:T(8,128)S(1)} collective-permute-done((f32[256,128]{1,0:T(8,128)S(1)}, f32[256,128]{1,0:T(8,128)S(1)}, u32[]{:S(2)}, u32[]{:S(2)}) %collective-permute-start.19) | collective-permute-done | bytes 131104 | tf_op jit(solution)/shard_map/ppermute | solution.py:235
  177.8 5.0 %gram_next.5 = (f32[2,136,128]{2,1,0:T(8,128)S(1)}, f32[4096,128]{1,0:T(8,128)S(1)}, f32[4096,128]{1,0:T(8,128)S(1)}) custom-call(s32[2]{0:T(128)S(1)} %add_convert_fusion.flag_ref, f32[4096,128]{1,0:T(8,128)S(1)} %get-tuple-element.57.first_ref, f32[4096,128]{1,0:T(8,128)S(1)} %get-tuple-element.58.last_ref, f32[4096,128]{1,0:T(8,128)S(1)} %get-tuple-element.59.b0_ref, ...), custom_call_target="tpu_custom_call" | custom-call | flops 60000002048 | bytes 1048576 | tf_op jit(solution)/shard_map/gram_next/pallas_call | solution.py:115
  184.3 3.9 %collective-permute-start.21 = (f32[2,136,128]{2,1,0:T(8,128)S(1)}, f32[2,136,128]{2,1,0:T(8,128)S(1)}, u32[]{:S(2)}, u32[]{:S(2)}) collective-permute-start(f32[2,136,128]{2,1,0:T(8,128)S(1)} %add.15.refs_0_), channel_id=1, source_target_pairs={{0,2},{1,3},{2,0},{3,1},{4,6},{5,7},{6,4},{7,5},{8,10},{9,11},{10,... | collective-permute-start | bytes 417800 | tf_op jit(solution)/shard_map/ppermute | solution.py:242
  188.3 4.0 %collective-permute-done.21.refs_1_ = f32[2,136,128]{2,1,0:T(8,128)S(1)} collective-permute-done((f32[2,136,128]{2,1,0:T(8,128)S(1)}, f32[2,136,128]{2,1,0:T(8,128)S(1)}, u32[]{:S(2)}, u32[]{:S(2)}) %collective-permute-start.21) | collective-permute-done | bytes 139296 | tf_op jit(solution)/shard_map/ppermute | solution.py:242
  192.2 7.1 %polar.7 = (f32[2,256,256]{2,1,0:T(8,128)S(1)}, f32[256,128]{1,0:T(8,128)}, f32[256,128]{1,0:T(8,128)}) custom-call(s32[2]{0:T(128)S(1)} %add_convert_fusion.flag_ref, f32[2,136,128]{2,1,0:T(8,128)S(1)} %add.15.refs_0_, f32[2,136,128]{2,1,0:T(8,128)S(1)} %collective-permute-done.21.refs_1_), custom_call_target="tpu_custom_call" | custom-call | flops 5000000000 | bytes 1048576 | tf_op jit(solution)/shard_map/polar/pallas_call | solution.py:166
  199.4 5.6 %rotate.5 = f32[4096,512]{1,0:T(8,128)} custom-call(f32[4096,128]{1,0:T(8,128)S(1)} %get-tuple-element.63.t0_ref, f32[4096,128]{1,0:T(8,128)S(1)} %get-tuple-element.59.b0_ref, f32[4096,128]{1,0:T(8,128)S(1)} %get-tuple-element.60.t1_ref, f32[4096,128]{1,0:T(8,128)S(1)} %get-tuple-element.64.b1_ref, f32[2,256,256]{2,1,0:T(8,128)S(1)} %get-tuple-element.66.q_ref), custom_call_target="tpu_custom_call" | custom-call | flops 5000000000 | bytes 1048576 | tf_op jit(solution)/shard_map/rotate/pallas_call | solution.py:199
  (43 shorter events, 47.7 us)
Async XLA Ops:
  4.1 3.4 %copy-start = (f32[4096,512]{1,0:T(8,128)}, f32[4096,512]{1,0:T(8,128)S(1)}, u32[]{:S(2)}) copy-start(f32[4096,512]{1,0:T(8,128)S(1)} %get-tuple-element.36.x_ref) | copy-start | bytes 25165828
  7.5 1.4 collective-permute-start
  8.9 7.9 %collective-permute-start.1 = (f32[2,136,128]{2,1,0:T(8,128)S(1)}, f32[2,136,128]{2,1,0:T(8,128)S(1)}, u32[]{:S(2)}, u32[]{:S(2)}) collective-permute-start(f32[2,136,128]{2,1,0:T(8,128)S(1)} %add.12.refs_0_), channel_id=1, source_target_pairs={{0,2},{1,3},{2,0},{3,1},{4,6},{5,7},{6,4},{7,5},{8,10},{9,11},{10,... | collective-permute-start | bytes 417800 | tf_op jit(solution)/shard_map/ppermute | solution.py:242
  16.8 7.1 %copy-start.1 = (f32[4096,512]{1,0:T(8,128)S(1)}, f32[4096,512]{1,0:T(8,128)}, u32[]{:S(2)}) copy-start(f32[4096,512]{1,0:T(8,128)} %copy-done) | copy-start | bytes 25165828
  26.9 50.4 %collective-permute-start.2 = (f32[4096,128]{1,0:T(8,128)S(1)}, f32[4096,128]{1,0:T(8,128)S(1)}, u32[]{:S(2)}, u32[]{:S(2)}) collective-permute-start(f32[4096,128]{1,0:T(8,128)S(1)} %get-tuple-element.40.last_ref.rest_1_), channel_id=1, source_target_pairs={{0,4},{4,8},{8,12},{12,16},{16,20},{20,24},{24,28},{28,32},{32,36}... | collective-permute-start | bytes 6291464 | tf_op jit(solution)/shard_map/ppermute | solution.py:235
  29.6 54.7 %collective-permute-start.3 = (f32[4096,128]{1,0:T(8,128)S(1)}, f32[4096,128]{1,0:T(8,128)S(1)}, u32[]{:S(2)}, u32[]{:S(2)}) collective-permute-start(f32[4096,128]{1,0:T(8,128)S(1)} %get-tuple-element.39.first_ref.rest_0_), channel_id=1, source_target_pairs={{4,0},{8,4},{12,8},{16,12},{20,16},{24,20},{28,24},{32,28},{36,32}... | collective-permute-start | bytes 6291464 | tf_op jit(solution)/shard_map/ppermute | solution.py:235
  35.7 86.6 %collective-permute-start.8 = (f32[4096,128]{1,0:T(8,128)S(1)}, f32[4096,128]{1,0:T(8,128)S(1)}, u32[]{:S(2)}, u32[]{:S(2)}) collective-permute-start(f32[4096,128]{1,0:T(8,128)S(1)} %get-tuple-element.42.t1_ref), channel_id=1, source_target_pairs={{0,4},{4,8},{8,12},{12,16},{16,20},{20,24},{24,28},{28,32},{32,36}... | collective-permute-start | bytes 6291464 | tf_op jit(solution)/shard_map/ppermute | solution.py:235
  42.7 86.0 %collective-permute-start.9 = (f32[4096,128]{1,0:T(8,128)S(1)}, f32[4096,128]{1,0:T(8,128)S(1)}, u32[]{:S(2)}, u32[]{:S(2)}) collective-permute-start(f32[4096,128]{1,0:T(8,128)S(1)} %get-tuple-element.41.b0_ref), channel_id=1, source_target_pairs={{4,0},{8,4},{12,8},{16,12},{20,16},{24,20},{28,24},{32,28},{36,32}... | collective-permute-start | bytes 6291464 | tf_op jit(solution)/shard_map/ppermute | solution.py:235
  87.8 1.4 collective-permute-start.4
  89.2 6.2 %collective-permute-start.6 = (f32[2,136,128]{2,1,0:T(8,128)S(1)}, f32[2,136,128]{2,1,0:T(8,128)S(1)}, u32[]{:S(2)}, u32[]{:S(2)}) collective-permute-start(f32[2,136,128]{2,1,0:T(8,128)S(1)} %add.13.refs_0_), channel_id=1, source_target_pairs={{0,22},{1,23},{2,20},{3,21},{124,106},{125,107},{126,104},{127,105}} | collective-permute-start | bytes 417800 | tf_op jit(solution)/shard_map/ppermute | solution.py:247
  89.9 9.5 %collective-permute-start.5 = (f32[2,136,128]{2,1,0:T(8,128)S(1)}, f32[2,136,128]{2,1,0:T(8,128)S(1)}, u32[]{:S(2)}, u32[]{:S(2)}) collective-permute-start(f32[2,136,128]{2,1,0:T(8,128)S(1)} %add.13.refs_0_), channel_id=1, source_target_pairs={{4,6},{5,7},{6,4},{7,5},{8,10},{9,11},{10,8},{11,9},{12,14},{13,15... | collective-permute-start | bytes 417800 | tf_op jit(solution)/shard_map/ppermute | solution.py:248
  95.4 4.0 %collective-permute-start.7 = (f32[2,136,128]{2,1,0:T(8,128)S(1)}, f32[2,136,128]{2,1,0:T(8,128)S(1)}, u32[]{:S(2)}, u32[]{:S(2)}) collective-permute-start(f32[2,136,128]{2,1,0:T(8,128)S(1)} %collective-permute-done.6), channel_id=1, source_target_pairs={{20,0},{21,1},{22,2},{23,3},{104,124},{105,125},{106,126},{107,127}} | collective-permute-start | bytes 417800 | tf_op jit(solution)/shard_map/ppermute | solution.py:249
  105.9 22.8 %collective-permute-start.10 = (f32[256,128]{1,0:T(8,128)S(1)}, f32[256,128]{1,0:T(8,128)S(1)}, u32[]{:S(2)}, u32[]{:S(2)}) collective-permute-start(f32[256,128]{1,0:T(8,128)S(1)} %get-tuple-element.51), channel_id=1, source_target_pairs={{0,4},{4,8},{8,12},{12,16},{16,20},{20,24},{24,28},{28,32},{32,36}... | collective-permute-start | bytes 393224 | tf_op jit(solution)/shard_map/ppermute | solution.py:235
  107.8 22.6 %collective-permute-start.11 = (f32[256,128]{1,0:T(8,128)S(1)}, f32[256,128]{1,0:T(8,128)S(1)}, u32[]{:S(2)}, u32[]{:S(2)}) collective-permute-start(f32[256,128]{1,0:T(8,128)S(1)} %get-tuple-element.52), channel_id=1, source_target_pairs={{4,0},{8,4},{12,8},{16,12},{20,16},{24,20},{28,24},{32,28},{36,32}... | collective-permute-start | bytes 393224 | tf_op jit(solution)/shard_map/ppermute | solution.py:235
  115.8 62.0 %collective-permute-start.16 = (f32[4096,128]{1,0:T(8,128)S(1)}, f32[4096,128]{1,0:T(8,128)S(1)}, u32[]{:S(2)}, u32[]{:S(2)}) collective-permute-start(f32[4096,128]{1,0:T(8,128)S(1)} %get-tuple-element.50.t1_ref), channel_id=1, source_target_pairs={{0,4},{4,8},{8,12},{12,16},{16,20},{20,24},{24,28},{28,32},{32,36}... | collective-permute-start | bytes 6291464 | tf_op jit(solution)/shard_map/ppermute | solution.py:235
  122.3 55.6 %collective-permute-start.17 = (f32[4096,128]{1,0:T(8,128)S(1)}, f32[4096,128]{1,0:T(8,128)S(1)}, u32[]{:S(2)}, u32[]{:S(2)}) collective-permute-start(f32[4096,128]{1,0:T(8,128)S(1)} %get-tuple-element.49.b0_ref), channel_id=1, source_target_pairs={{4,0},{8,4},{12,8},{16,12},{20,16},{24,20},{28,24},{32,28},{36,32}... | collective-permute-start | bytes 6291464 | tf_op jit(solution)/shard_map/ppermute | solution.py:235
  135.4 1.4 collective-permute-start.12
  136.9 6.8 %collective-permute-start.14 = (f32[2,136,128]{2,1,0:T(8,128)S(1)}, f32[2,136,128]{2,1,0:T(8,128)S(1)}, u32[]{:S(2)}, u32[]{:S(2)}) collective-permute-start(f32[2,136,128]{2,1,0:T(8,128)S(1)} %add.14.refs_0_), channel_id=1, source_target_pairs={{0,22},{1,23},{2,20},{3,21},{124,106},{125,107},{126,104},{127,105}} | collective-permute-start | bytes 417800 | tf_op jit(solution)/shard_map/ppermute | solution.py:247
  137.5 10.1 %collective-permute-start.13 = (f32[2,136,128]{2,1,0:T(8,128)S(1)}, f32[2,136,128]{2,1,0:T(8,128)S(1)}, u32[]{:S(2)}, u32[]{:S(2)}) collective-permute-start(f32[2,136,128]{2,1,0:T(8,128)S(1)} %add.14.refs_0_), channel_id=1, source_target_pairs={{4,6},{5,7},{6,4},{7,5},{8,10},{9,11},{10,8},{11,9},{12,14},{13,15... | collective-permute-start | bytes 417800 | tf_op jit(solution)/shard_map/ppermute | solution.py:248
  143.7 4.0 %collective-permute-start.15 = (f32[2,136,128]{2,1,0:T(8,128)S(1)}, f32[2,136,128]{2,1,0:T(8,128)S(1)}, u32[]{:S(2)}, u32[]{:S(2)}) collective-permute-start(f32[2,136,128]{2,1,0:T(8,128)S(1)} %collective-permute-done.14), channel_id=1, source_target_pairs={{20,0},{21,1},{22,2},{23,3},{104,124},{105,125},{106,126},{107,127}} | collective-permute-start | bytes 417800 | tf_op jit(solution)/shard_map/ppermute | solution.py:249
  154.1 17.3 %collective-permute-start.18 = (f32[256,128]{1,0:T(8,128)S(1)}, f32[256,128]{1,0:T(8,128)S(1)}, u32[]{:S(2)}, u32[]{:S(2)}) collective-permute-start(f32[256,128]{1,0:T(8,128)S(1)} %get-tuple-element.61), channel_id=1, source_target_pairs={{0,4},{4,8},{8,12},{12,16},{16,20},{20,24},{24,28},{28,32},{32,36}... | collective-permute-start | bytes 393224 | tf_op jit(solution)/shard_map/ppermute | solution.py:235
  156.1 21.8 %collective-permute-start.19 = (f32[256,128]{1,0:T(8,128)S(1)}, f32[256,128]{1,0:T(8,128)S(1)}, u32[]{:S(2)}, u32[]{:S(2)}) collective-permute-start(f32[256,128]{1,0:T(8,128)S(1)} %get-tuple-element.62), channel_id=1, source_target_pairs={{4,0},{8,4},{12,8},{16,12},{20,16},{24,20},{28,24},{32,28},{36,32}... | collective-permute-start | bytes 393224 | tf_op jit(solution)/shard_map/ppermute | solution.py:235
  182.9 1.4 collective-permute-start.20
  184.3 7.9 %collective-permute-start.21 = (f32[2,136,128]{2,1,0:T(8,128)S(1)}, f32[2,136,128]{2,1,0:T(8,128)S(1)}, u32[]{:S(2)}, u32[]{:S(2)}) collective-permute-start(f32[2,136,128]{2,1,0:T(8,128)S(1)} %add.15.refs_0_), channel_id=1, source_target_pairs={{0,2},{1,3},{2,0},{3,1},{4,6},{5,7},{6,4},{7,5},{8,10},{9,11},{10,... | collective-permute-start | bytes 417800 | tf_op jit(solution)/shard_map/ppermute | solution.py:242
